TPU v7x, 128 devices: a whole 4x4x4 slice. The times are simulated.
128 devices in a mesh: row: 16 (over x, y_lo, core), col: 8 (over y_hi, z).
Axes of the slice: x: 4, y: 4 (y_hi: 2, y_lo: 2; y = y_hi * 2 + y_lo), z: 4, core: 2. Of those that a mesh axis runs over, the one named last changes fastest.
Arguments:
- vision_tokens: bfloat16 [2048, 8192], P(('row', 'col')), may hold values from -6 to 6
- image_counts: int32 [64], replicated, may hold values from 1 to 32, 1024 in all
- image_owner: int32 [128], replicated, may hold values from 0 to 127, each once
- gate_weight: bfloat16 [8192, 14336], P('row', 'col'), may hold values from -0.0625 to 0.0625
- up_weight: bfloat16 [8192, 14336], P('row', 'col'), may hold values from -0.0625 to 0.0625
- down_weight: bfloat16 [14336, 8192], P('col', 'row'), may hold values from -0.046875 to 0.046875
- out_grad: bfloat16 [1024, 8192], P('col', 'row'), may hold values from -0.19921875 to 0.19921875
Outputs:
- layer_out: bfloat16 [1024, 8192], P('col', 'row')
- grad_gate: float32 [8192, 14336], P('row', 'col')
- grad_up: float32 [8192, 14336], P('row', 'col')
- grad_down: float32 [14336, 8192], P('col', 'row')
Inputs may be any that keep to these rules, and one draw needn't show every extreme that they name: `image_counts`: every image has 1 to 32 tokens, together 1024; some image has exactly 32. `image_owner`: each encoder device, numbered row index * 8 + col index, appears once; so every device holds at most 16 tokens, and one holds exactly 16.
All inputs are finite; a program needn't handle non-finite values.
Results may differ from a plain program's by a relative error of at most 0.0049.
Values may be sent and summed in bfloat16 or wider, within the bound.
A program may use at most 128 MiB of HBM per device.

v0:
```python
import jax
import jax.numpy as jnp
from jax import lax
from jax.sharding import PartitionSpec as P


def token_place(image_counts, image_owner, total):
    position = jnp.arange(total, dtype=jnp.int32)
    ends = jnp.cumsum(image_counts)
    starts = ends - image_counts
    member = ((position[:, None] >= starts[None, :]) & (position[:, None] < ends[None, :])).astype(
        jnp.int32
    )
    count = jnp.sum(member * image_counts[None, :], axis=1)
    begin = jnp.sum(member * starts[None, :], axis=1)
    owner_first = jnp.sum(member * image_owner[0::2][None, :], axis=1)
    owner_second = jnp.sum(member * image_owner[1::2][None, :], axis=1)
    first = (count + 1) // 2
    within = position - begin
    second = (within >= first).astype(jnp.int32)
    slot = within - second * first
    owner = jnp.where(second > 0, owner_second, owner_first)
    return (owner, slot)


def pair_grads(gate, up, hidden_grad):
    sigma = jax.nn.sigmoid(gate)
    gate_grad = hidden_grad * up * sigma * (1.0 + gate * (1.0 - sigma))
    up_grad = hidden_grad * gate * sigma
    return jnp.concatenate((gate_grad, up_grad), axis=1).astype(jnp.bfloat16)


def local(vision_tokens, image_counts, image_owner, gate_weight, up_weight, down_weight, out_grad):
    slots = vision_tokens.shape[0]
    row_count = lax.axis_size("row")
    col_count = lax.axis_size("col")
    token_total = out_grad.shape[0] * col_count
    owner, slot = token_place(image_counts, image_owner, token_total)
    owner_row = owner // col_count
    owner_col = owner % col_count
    received = lax.all_to_all(vision_tokens, "row", split_axis=1, concat_axis=0, tiled=True)
    pooled, cotangent = (
        lax.all_gather(received, "col", axis=0, tiled=True),
        lax.all_gather(out_grad, "col", axis=0, tiled=True),
    )
    pool_index = owner_col * (row_count * slots) + owner_row * slots + slot
    inputs = jnp.take(pooled, pool_index, axis=0)
    width = gate_weight.shape[1]
    both_weights = jnp.concatenate((gate_weight, up_weight), axis=1)
    contract_last = (((1,), (1,)), ((), ()))
    contract_first = (((0,), (0,)), ((), ()))
    block = inputs
    gate_up = lax.psum_scatter(
        jnp.dot(block, both_weights, preferred_element_type=jnp.float32),
        "row",
        scatter_dimension=0,
        tiled=True,
    )
    gate = gate_up[:, :width]
    up = gate_up[:, width:]
    hidden_part = (gate * jax.nn.sigmoid(gate) * up).astype(jnp.bfloat16)
    hidden = lax.all_gather(hidden_part, "row", axis=0, tiled=True)
    block = cotangent
    hidden_grad = lax.psum_scatter(
        lax.dot_general(block, down_weight, contract_last, preferred_element_type=jnp.float32),
        "row",
        scatter_dimension=0,
        tiled=True,
    )
    grads_part = pair_grads(gate, up, hidden_grad)
    pre_grads = lax.all_gather(grads_part, "row", axis=0, tiled=True)
    block = hidden
    layer_out = lax.psum_scatter(
        jnp.dot(block, down_weight, preferred_element_type=jnp.float32),
        "col",
        scatter_dimension=0,
        tiled=True,
    ).astype(jnp.bfloat16)
    grad_down = lax.dot_general(
        hidden, cotangent, contract_first, preferred_element_type=jnp.float32
    )
    both = lax.dot_general(inputs, pre_grads, contract_first, preferred_element_type=jnp.float32)
    return (layer_out, both[:, :width], both[:, width:], grad_down)


def solution(mesh):
    in_specs = (
        P(("row", "col"), None),
        P(),
        P(),
        P("row", "col"),
        P("row", "col"),
        P("col", "row"),
        P("col", "row"),
    )
    out_specs = (P("col", "row"), P("row", "col"), P("row", "col"), P("col", "row"))
    return jax.shard_map(local, mesh=mesh, in_specs=in_specs, out_specs=out_specs, check_vma=False)
```

profile of v0, /device:TPU:1, one launch (start us, length us, event | category | flops | bytes accessed | tf_op | source)
XLA Modules:
  0.0 550.5 jit_solution(6683519192541431481)
XLA Ops:
  7.2 0.7 all-gather.9.cloned.1.call-update
  8.0 1.0 copy.19
  8.9 14.1 %all_to_all.19 = bf16[16,16,512]{2,0,1:T(8,128)(2,1)} all-to-all(bf16[16,16,512]{2,0,1:T(8,128)(2,1)S(1)} %bitcast.21), channel_id=1, replica_groups=mesh['row'=16,'col'=8] {'row'}, dimensions={1} | all-to-all | bytes 524288 | tf_op jit(solution)/shard_map/all_to_all | solution.py:41
  23.1 35.7 %all-gather.9.cloned.1.call-done = bf16[1024,512]{1,0:T(8,128)(2,1)} async-done(((bf16[128,512]{1,0:T(8,128)(2,1)}), bf16[1024,512]{1,0:T(8,128)(2,1)}) %all-gather.9.cloned.1.call-update) | async-done | bytes 1048592 | tf_op jit(solution)/shard_map/all_gather | solution.py:44
  58.8 6.2 %fusion.26 = f32[1024,1792]{1,0:T(8,128)} fusion(bf16[1024,512]{1,0:T(8,128)(2,1)} %all-gather.9.cloned.1.call-done, bf16[1792,512]{1,0:T(8,128)(2,1)S(1)} %copy-done), kind=kOutput, calls=%fused_computation.70 | convolution fusion | flops 1879048192 | bytes 10223616 | tf_op jit(solution)/shard_map/dot_general | solution.py:65
  65.2 0.6 copy-done.3
  65.7 0.2 slice.18
  65.9 0.2 slice.19
  66.4 0.2 select_reduce_fusion.3
  66.7 48.2 %all-gather.5.cloned.1.call-done = bf16[2048,512]{1,0:T(8,128)(2,1)} async-done(((bf16[256,512]{1,0:T(8,128)(2,1)}), bf16[2048,512]{1,0:T(8,128)(2,1)}) %all-gather.5.cloned.1.call-update) | async-done | bytes 2097168 | tf_op jit(solution)/shard_map/all_gather | solution.py:43
  114.9 5.8 %gather_fusion = bf16[1024,512]{1,0:T(8,128)(2,1)S(1)} fusion(bf16[2048,512]{1,0:T(8,128)(2,1)} %all-gather.5.cloned.1.call-done, s32[1024]{0:T(1024)S(1)} %broadcast_clamp_fusion), kind=kCustom, calls=%fused_computation | custom fusion | bytes 2101248 | tf_op jit(solution)/shard_map/jit(_take)/gather | solution.py:47
  120.8 9.7 %fusion = f32[1024,3584]{1,0:T(8,128)} fusion(bf16[512,1792]{1,0:T(8,128)(2,1)} %param.11, bf16[512,1792]{1,0:T(8,128)(2,1)} %param.10, bf16[1024,512]{1,0:T(8,128)(2,1)S(1)} %gather_fusion, pred[1024]{0:T(1024)(128)(4,1)S(1)} %compare_and_fusion), kind=kOutput, calls=%fused_computation.1 | convolution fusion | flops 3765960704 | bytes 19399680 | tf_op jit(solution)/shard_map/dot_general | solution.py:54
  130.5 70.7 %reduce-scatter.8.cloned.1.call-done = f32[64,1792]{1,0:T(8,128)} async-done(((f32[1024,1792]{1,0:T(8,128)}), f32[64,1792]{1,0:T(8,128)}) %reduce-scatter.8.cloned.1.call-update) | async-done | bytes 458768 | tf_op jit(solution)/shard_map/reduce_scatter | solution.py:64
  201.3 163.7 %reduce-scatter.4.cloned.1.call-done = f32[64,3584]{1,0:T(8,128)} async-done(((f32[1024,3584]{1,0:T(8,128)}), f32[64,3584]{1,0:T(8,128)}) %reduce-scatter.4.cloned.1.call-update) | async-done | bytes 917520 | tf_op jit(solution)/shard_map/reduce_scatter | solution.py:53
  365.0 2.2 multiply_convert_fusion.1
  367.3 37.2 %all-gather.7.cloned.1.call-done = bf16[1024,1792]{1,0:T(8,128)(2,1)} async-done(((bf16[64,1792]{1,0:T(8,128)(2,1)}), bf16[1024,1792]{1,0:T(8,128)(2,1)}) %all-gather.7.cloned.1.call-update) | async-done | bytes 3670032 | tf_op jit(solution)/shard_map/all_gather | solution.py:62
  404.5 5.4 fusion.25
  410.0 0.8 pad_maximum_fusion
  410.8 6.3 %fusion.27 = f32[1792,512]{1,0:T(8,128)} fusion(bf16[1024,1792]{1,0:T(8,128)(2,1)} %all-gather.7.cloned.1.call-done, bf16[1024,512]{1,0:T(8,128)(2,1)} %all-gather.9.cloned.1.call-done), kind=kOutput, calls=%fused_computation.71 | convolution fusion | flops 1879048192 | bytes 8388608 | tf_op jit(solution)/shard_map/dot_general | solution.py:79
  417.1 66.5 %reduce-scatter.6.cloned.1.call-done = f32[128,512]{1,0:T(8,128)} async-done(((f32[1024,512]{1,0:T(8,128)}), f32[128,512]{1,0:T(8,128)}) %reduce-scatter.6.cloned.1.call-update) | async-done | bytes 262160 | tf_op jit(solution)/shard_map/reduce_scatter | solution.py:73
  483.5 1.6 convert_element_type.25
  485.2 48.3 %all-gather.11.cloned.1.call-done = bf16[1024,3584]{1,0:T(8,128)(2,1)} async-done(((bf16[64,3584]{1,0:T(8,128)(2,1)}), bf16[1024,3584]{1,0:T(8,128)(2,1)}) %all-gather.11.cloned.1.call-update) | async-done | bytes 7340048 | tf_op jit(solution)/shard_map/all_gather | solution.py:71
  533.5 6.5 %fusion.4 = f32[512,3584]{1,0:T(8,128)S(1)} fusion(bf16[1024,3584]{1,0:T(8,128)(2,1)} %all-gather.11.cloned.1.call-done, bf16[1024,512]{1,0:T(8,128)(2,1)S(1)} %gather_fusion, pred[1024]{0:T(1024)(128)(4,1)S(1)} %compare_and_fusion), kind=kOutput, calls=%fused_computation.11 | convolution fusion | flops 3758620672 | bytes 15729664 | tf_op jit(solution)/shard_map/dot_general | solution.py:82
  540.1 3.6 fusion.24
  (28 shorter events, 0.8 us)
Async XLA Ops:
  7.2 51.7 %copy-start = (bf16[1792,512]{1,0:T(8,128)(2,1)S(1)}, bf16[1792,512]{1,0:T(8,128)(2,1)}, u32[]{:S(2)}) copy-start(bf16[1792,512]{1,0:T(8,128)(2,1)} %param.12) | copy-start | bytes 5505028
  7.2 51.7 %all-gather.9.cloned.1.call-start = ((), (), s32[]{:S(2)}) async-start(), calls=%async_computation.8 | async-start | bytes 1179648 | tf_op jit(solution)/shard_map/all_gather | solution.py:44
  7.9 107.0 %all-gather.5.cloned.1.call-start = ((), (), s32[]{:S(2)}) async-start(), calls=%async_computation.4 | async-start | bytes 2359296 | tf_op jit(solution)/shard_map/all_gather | solution.py:43
  23.1 178.2 %reduce-scatter.8.cloned.1.call-start = ((), (), s32[]{:S(2)}) async-start(), calls=%async_computation.9 | async-start | bytes 7798784 | tf_op jit(solution)/shard_map/reduce_scatter | solution.py:64
  65.1 0.7 copy-start.3
  65.1 1.0 copy-start.2
  65.1 299.9 %reduce-scatter.4.cloned.1.call-start = ((), (), s32[]{:S(2)}) async-start(), calls=%async_computation.5 | async-start | bytes 15597568 | tf_op jit(solution)/shard_map/reduce_scatter | solution.py:53
  130.5 274.0 %all-gather.7.cloned.1.call-start = ((), (), s32[]{:S(2)}) async-start(), calls=%async_computation.6 | async-start | bytes 3899392 | tf_op jit(solution)/shard_map/all_gather | solution.py:62
  367.2 116.3 %reduce-scatter.6.cloned.1.call-start = ((), (), s32[]{:S(2)}) async-start(), calls=%async_computation.7 | async-start | bytes 2359296 | tf_op jit(solution)/shard_map/reduce_scatter | solution.py:73
  409.9 123.6 %all-gather.11.cloned.1.call-start = ((), (), s32[]{:S(2)}) async-start(), calls=%async_computation.10 | async-start | bytes 7798784 | tf_op jit(solution)/shard_map/all_gather | solution.py:71
  540.0 3.6 copy-start.1
Sparse Core Ops, SparseCore 0:
  10.4 48.4 all-gather.8
  61.2 53.6 all-gather.4
  117.3 83.8 reduce-scatter.7
  203.5 161.4 reduce-scatter.3
  367.4 37.0 all-gather.6
  410.1 73.4 reduce-scatter.5
  485.8 47.6 all-gather.10
where the time goes:
time: 551 us
  waiting for transfers between devices  471 us (85%)
  matrix products  34.1 us (6%)
  between operations  14.2 us (3%)
  blocking collectives  14.1 us (3%)
  local copies, waits for them, and re-layouts  11.4 us (2%)
    reduce_scatter x1, waiting for transfers between devices, local(): lax.psum_scatter(jnp.dot(block, both_weights, preferred_element_type=jnp....  164 us
    reduce_scatter x1, waiting for transfers between devices, local(): lax.psum_scatter(lax.dot_general(block, down_weight, contract_last, prefe...  70.7 us
    reduce_scatter x1, waiting for transfers between devices, local(): lax.psum_scatter(jnp.dot(block, down_weight, preferred_element_type=jnp.f...  66.5 us
    all_gather x1, waiting for transfers between devices, local(): pre_grads = lax.all_gather(grads_part, 'row', axis=0, tiled=True)  48.3 us
    all_gather x1, waiting for transfers between devices, local(): lax.all_gather(received, 'col', axis=0, tiled=True)  48.2 us
    all_gather x1, waiting for transfers between devices, local(): hidden = lax.all_gather(hidden_part, 'row', axis=0, tiled=True)  37.2 us
    all_gather x1, waiting for transfers between devices, local(): lax.all_gather(out_grad, 'col', axis=0, tiled=True)  35.7 us
    all_to_all x1, blocking collectives, local(): lax.all_to_all(vision_tokens, 'row', split_axis=1, concat_axis=0, tiled=T...  14.1 us
  transfers between devices with their start and end apart: 7, of which 7 were waited for; matrix products, arithmetic and copies ran while one was open for 6% of the time, Pallas kernels for 0%

commit v1 on v0

v1 whole, which is shorter than its diff:
```python
import functools
import jax
import jax.numpy as jnp
from jax import lax
from jax.experimental import pallas as pl
from jax.experimental.pallas import tpu as pltpu
from jax.sharding import PartitionSpec as P

BF = jnp.bfloat16
F32 = jnp.float32
MESH = pl.DeviceIdType.MESH

CHUNKS = 8
HALF = 896
XW = 512
YW = HALF - XW

XD, XR, X2, XY, YY, YD, YR, Y2 = range(8)
AXY, AXP, AXM, AXF, AYP, AYM, AYF, AYY, CORE, Z1, Z2, Z3, YH = range(8, 21)
KINDS = 21


def token_place(image_counts, image_owner, total):
    position = jnp.arange(total, dtype=jnp.int32)
    ends = jnp.cumsum(image_counts)
    starts = ends - image_counts
    member = ((position[:, None] >= starts[None, :]) & (position[:, None] < ends[None, :])).astype(
        jnp.int32
    )
    count = jnp.sum(member * image_counts[None, :], axis=1)
    begin = jnp.sum(member * starts[None, :], axis=1)
    owner_first = jnp.sum(member * image_owner[0::2][None, :], axis=1)
    owner_second = jnp.sum(member * image_owner[1::2][None, :], axis=1)
    first = (count + 1) // 2
    within = position - begin
    second = (within >= first).astype(jnp.int32)
    slot = within - second * first
    owner = jnp.where(second > 0, owner_second, owner_first)
    return (owner, slot)


def rem(a, n):
    return lax.rem(a, n)


def main_kernel(
    x_ref, c_ref, wg_ref, wu_ref, wd_ref, wdo_ref,
    out_ref, o_ref,
    act, px, py,
    sxd, sxr, sx2, sxy, syy, syd, syr, sy2,
    rxd, rxr, rx2, rxy, ryy, ryd, ryr, ry2,
    lo, zs, rz, rh,
    ssem, rsem, osem,
):
    row = lax.axis_index("row")
    col = lax.axis_index("col")
    x, y, k = row // 4, rem(row // 2, 2), rem(row, 2)
    yh, z = col // 4, rem(col, 4)
    yo, ko, ho = 1 - y, 1 - k, 1 - yh

    def at_row(xx, yy, kk):
        return {"row": xx * 4 + yy * 2 + kk}

    def at_col(hh, zz):
        return {"col": hh * 4 + zz}

    far = rem(x + 2, 4)
    y_dev = at_row(x, yo, k)
    core_dev = at_row(x, y, ko)
    partners = [
        core_dev, y_dev, at_row(rem(x + 1, 4), y, k), at_row(rem(x + 3, 4), y, k),
        at_col(yh, rem(z + 1, 4)), at_col(yh, rem(z + 2, 4)), at_col(yh, rem(z + 3, 4)),
        at_col(ho, z),
    ]
    barrier = pltpu.get_barrier_semaphore()
    for dev in partners:
        pl.semaphore_signal(barrier, inc=1, device_id=dev, device_id_type=MESH)
    pl.semaphore_wait(barrier, len(partners))

    cx = pl.ds(pl.multiple_of(k * HALF, 128), XW)
    cy = pl.ds(pl.multiple_of(k * HALF + XW, 128), YW)
    cc = pl.ds(pl.multiple_of(k * HALF, 128), HALF)
    cp = pl.ds(pl.multiple_of(ko * HALF, 128), HALF)

    def copy(kind, t, src, dst, dev):
        return pltpu.make_async_remote_copy(
            src_ref=src, dst_ref=dst, send_sem=ssem.at[kind, t], recv_sem=rsem.at[kind, t],
            device_id=dev, device_id_type=MESH,
        )

    def sides(t):
        s = 1 - 2 * rem(t, 2)
        return rem(x + s + 4, 4), rem(x - s + 4, 4)

    def sends(t):
        ahead, back = sides(t)
        to_ahead, to_back = at_row(ahead, y, k), at_row(back, y, k)
        c = functools.partial
        return {
            XD: c(copy, XD, t, sxd.at[t], rxd.at[t], to_ahead),
            XR: c(copy, XR, t, sxr.at[t], rxr.at[t], to_back),
            X2: c(copy, X2, t, sx2.at[t], rx2.at[t], to_back),
            XY: c(copy, XY, t, sxy.at[t], rxy.at[t], y_dev),
            YY: c(copy, YY, t, syy.at[t], ryy.at[t], y_dev),
            YD: c(copy, YD, t, syd.at[t], ryd.at[t], to_ahead),
            YR: c(copy, YR, t, syr.at[t], ryr.at[t], to_back),
            Y2: c(copy, Y2, t, sy2.at[t], ry2.at[t], to_back),
            AXY: lambda: both(AXY, t, act.at[t, x, y, :, :, cx], y_dev),
            AXP: lambda: both(AXP, t, act.at[t, x, :, :, :, cx], to_ahead),
            AXM: lambda: both(AXM, t, act.at[t, x, :, :, :, cx], to_back),
            AXF: lambda: both(AXF, t, act.at[t, back, :, :, :, cx], to_ahead),
            AYP: lambda: both(AYP, t, act.at[t, x, y, :, :, cy], to_ahead),
            AYM: lambda: both(AYM, t, act.at[t, x, y, :, :, cy], to_back),
            AYF: lambda: both(AYF, t, act.at[t, back, y, :, :, cy], to_ahead),
            AYY: lambda: both(AYY, t, act.at[t, :, y, :, :, cy], y_dev),
            CORE: lambda: both(CORE, t, act.at[t, :, :, :, :, cc], core_dev),
            Z1: lambda: copy(Z1, t, lo.at[t, :, rem(z + 1, 4)], rz.at[t, 0], at_col(yh, rem(z + 1, 4))),
            Z2: lambda: copy(Z2, t, lo.at[t, :, rem(z + 2, 4)], rz.at[t, 1], at_col(yh, rem(z + 2, 4))),
            Z3: lambda: copy(Z3, t, lo.at[t, :, rem(z + 3, 4)], rz.at[t, 2], at_col(yh, rem(z + 3, 4))),
            YH: lambda: copy(YH, t, zs.at[t, ho], rh.at[t], at_col(ho, z)),
        }

    def both(kind, t, ref, dev):
        return copy(kind, t, ref, ref, dev)

    def landed(kind, t):
        ahead, back = sides(t)
        place = {
            XD: lambda: rxd.at[t], XR: lambda: rxr.at[t], X2: lambda: rx2.at[t], XY: lambda: rxy.at[t],
            YY: lambda: ryy.at[t], YD: lambda: ryd.at[t], YR: lambda: ryr.at[t], Y2: lambda: ry2.at[t],
            AXY: lambda: act.at[t, x, yo, :, :, cx],
            AXP: lambda: act.at[t, back, :, :, :, cx],
            AXM: lambda: act.at[t, ahead, :, :, :, cx],
            AXF: lambda: act.at[t, far, :, :, :, cx],
            AYP: lambda: act.at[t, back, y, :, :, cy],
            AYM: lambda: act.at[t, ahead, y, :, :, cy],
            AYF: lambda: act.at[t, far, y, :, :, cy],
            AYY: lambda: act.at[t, :, yo, :, :, cy],
            CORE: lambda: act.at[t, :, :, :, :, cp],
            Z1: lambda: rz.at[t, 0], Z2: lambda: rz.at[t, 1], Z3: lambda: rz.at[t, 2],
            YH: lambda: rh.at[t],
        }[kind]()
        return copy(kind, t, place, place, y_dev)

    def start(t, *kinds):
        table = sends(t)
        for kind in kinds:
            table[kind]().start()

    def arrive(t, *kinds):
        for kind in kinds:
            landed(kind, t).wait_recv()

    def s0(t):
        b = rem(t, 4)
        ahead, _ = sides(t)
        x_t = x_ref[pl.ds(pl.multiple_of(t * 128, 128), 128), :]
        c_t = c_ref[:, pl.ds(pl.multiple_of(t * 16, 16), 16), :].reshape(128, 1024)
        for m in range(3):
            if m == 0:
                g = jnp.dot(x_t, wg_ref[...], preferred_element_type=F32)
            elif m == 1:
                g = jnp.dot(x_t, wu_ref[...], preferred_element_type=F32)
            else:
                g = lax.dot_general(c_t, wd_ref[...], (((1,), (1,)), ((), ())), preferred_element_type=F32)
            px[b, :, m] = g[:, :XW].reshape(4, 32, XW)
            gy = g[:, XW:].reshape(4, 2, 16, YW)
            for yy in range(2):
                py[b, yy, :, m] = gy[:, yy]
        sxd[t] = px[b, ahead].astype(BF)
        sxr[t] = px[b, far].astype(BF)
        start(t, XD, XR)
        syy[t] = py[b, yo].astype(BF)
        start(t, YY)

    def s1(t):
        b = rem(t, 4)
        ahead, back = sides(t)
        arrive(t, XR)
        sx2[t] = (px[b, back] + rxr[t].astype(F32)).astype(BF)
        start(t, X2)
        arrive(t, YY)
        py[b, y] = py[b, y] + ryy[t].astype(F32)
        syd[t] = py[b, y, ahead].astype(BF)
        syr[t] = py[b, y, far].astype(BF)
        start(t, YD, YR)

    def s2(t):
        b = rem(t, 4)
        _, back = sides(t)
        arrive(t, XD, X2)
        px[b, x] = px[b, x] + rxd[t].astype(F32) + rx2[t].astype(F32)
        sxy[t] = px[b, x, :, pl.ds(pl.multiple_of(yo * 16, 16), 16), :].astype(BF)
        start(t, XY)
        arrive(t, YR)
        sy2[t] = (py[b, y, back] + ryr[t].astype(F32)).astype(BF)
        start(t, Y2)

    def activate(t, full, cols):
        gate, up, hg = full[0], full[1], full[2]
        sigma = jax.nn.sigmoid(gate)
        act[t, x, y, 0, :, cols] = (gate * sigma * up).astype(BF)
        act[t, x, y, 1, :, cols] = (hg * up * sigma * (1.0 + gate * (1.0 - sigma))).astype(BF)
        act[t, x, y, 2, :, cols] = (hg * gate * sigma).astype(BF)

    def s3(t):
        b = rem(t, 4)
        arrive(t, XY)
        activate(t, px[b, x, :, pl.ds(pl.multiple_of(y * 16, 16), 16), :] + rxy[t].astype(F32), cx)
        start(t, AXY)
        arrive(t, YD, Y2)
        activate(t, py[b, y, x] + ryd[t].astype(F32) + ry2[t].astype(F32), cy)
        start(t, AYP, AYM)

    def s4(t):
        arrive(t, AXY)
        start(t, AXP, AXM)
        arrive(t, AYP)
        start(t, AYF)
        arrive(t, AYM)

    def s5(t):
        arrive(t, AXP)
        start(t, AXF)
        arrive(t, AXM)
        arrive(t, AYF)
        start(t, AYY)

    def s6(t):
        arrive(t, AXF, AYY)
        start(t, CORE)

    def s7(t):
        arrive(t, CORE)
        pltpu.make_async_copy(act.at[t], o_ref.at[t], osem.at[t]).start()
        hidden = act[t, :, :, 0].reshape(128, 2 * HALF)
        part = jnp.dot(hidden, wdo_ref[...], preferred_element_type=F32)
        lo[t] = part.reshape(2, 4, 16, 512)
        start(t, Z1, Z2, Z3)

    def s8(t):
        arrive(t, Z1, Z2, Z3)
        zs[t] = lo[t, :, z] + rz[t, 0] + rz[t, 1] + rz[t, 2]
        start(t, YH)

    def s9(t):
        arrive(t, YH)
        out_ref[pl.ds(pl.multiple_of(t * 16, 16), 16), :] = (zs[t, yh] + rh[t]).astype(BF)

    stages = [s0, s1, s2, s3, s4, s5, s6, s7, s8, s9]

    def step(n, carry):
        for lag, stage in enumerate(stages):
            t = n - lag

            @pl.when((t >= 0) & (t < CHUNKS))
            def _():
                stage(t)

        return carry

    lax.fori_loop(0, CHUNKS + len(stages) - 1, step, 0)

    def finish(t, carry):
        table = sends(t)
        for kind in range(KINDS):
            table[kind]().wait_send()
        pltpu.make_async_copy(act.at[t], o_ref.at[t], osem.at[t]).wait()
        return carry

    lax.fori_loop(0, CHUNKS, finish, 0)


def main_call(x, c, wg, wu, wd, wdo):
    n = CHUNKS
    vm = lambda *s: pltpu.VMEM(s, BF)
    vf = lambda *s: pltpu.VMEM(s, F32)
    xb, xq, yb = (n, 3, 32, XW), (n, 3, 16, XW), (n, 3, 16, YW)
    moves = [vm(*xb), vm(*xb), vm(*xb), vm(*xq), vm(n, 4, 3, 16, YW), vm(*yb), vm(*yb), vm(*yb)]
    return pl.pallas_call(
        main_kernel,
        out_shape=(
            jax.ShapeDtypeStruct((128, 512), BF),
            jax.ShapeDtypeStruct((n, 4, 2, 3, 16, 2 * HALF), BF),
        ),
        in_specs=[pl.BlockSpec(memory_space=pltpu.VMEM)] * 6,
        out_specs=(pl.BlockSpec(memory_space=pltpu.VMEM), pl.BlockSpec(memory_space=pl.ANY)),
        scratch_shapes=[
            vm(n, 4, 2, 3, 16, 2 * HALF), vf(4, 4, 3, 32, XW), vf(4, 2, 4, 3, 16, YW),
            *moves, *moves,
            vf(n, 2, 4, 16, 512), vf(n, 2, 16, 512), vf(n, 3, 2, 16, 512), vf(n, 16, 512),
            pltpu.SemaphoreType.DMA((KINDS, n)), pltpu.SemaphoreType.DMA((KINDS, n)),
            pltpu.SemaphoreType.DMA((n,)),
        ],
        compiler_params=pltpu.CompilerParams(
            collective_id=0, has_side_effects=True, vmem_limit_bytes=58 << 20
        ),
        cost_estimate=pl.CostEstimate(flops=8 * 10**9, bytes_accessed=30 * 10**6, transcendentals=0),
        name="row_sums",
    )(x, c, wg, wu, wd, wdo)


def grads_kernel(x_ref, c_ref, h_ref, gg_ref, ug_ref, gate_ref, up_ref, down_ref, xt, cs):
    @pl.when(pl.program_id(0) == 0)
    def _():
        xt[...] = x_ref[...].T
        for t in range(CHUNKS):
            cs[pl.ds(t * 128, 128), :] = c_ref[:, t].reshape(128, 512)

    width = h_ref.shape[-1]
    gate_ref[...] = jnp.dot(xt[...], gg_ref[...].reshape(1024, width), preferred_element_type=F32)
    up_ref[...] = jnp.dot(xt[...], ug_ref[...].reshape(1024, width), preferred_element_type=F32)
    down_ref[...] = lax.dot_general(
        h_ref[...].reshape(1024, width), cs[...], (((0,), (0,)), ((), ())), preferred_element_type=F32
    )


def grads_call(x, c, o):
    width = 256
    n = CHUNKS
    part = lambda m: pl.BlockSpec((n, 4, 2, 1, 16, width), lambda j: (0, 0, 0, m, 0, j))
    return pl.pallas_call(
        grads_kernel,
        grid=(1792 // width,),
        out_shape=(
            jax.ShapeDtypeStruct((512, 1792), F32),
            jax.ShapeDtypeStruct((512, 1792), F32),
            jax.ShapeDtypeStruct((1792, 512), F32),
        ),
        in_specs=[
            pl.BlockSpec((1024, 512), lambda j: (0, 0)),
            pl.BlockSpec((8, n, 16, 512), lambda j: (0, 0, 0, 0)),
            part(0), part(1), part(2),
        ],
        out_specs=(
            pl.BlockSpec((512, width), lambda j: (0, j)),
            pl.BlockSpec((512, width), lambda j: (0, j)),
            pl.BlockSpec((width, 512), lambda j: (j, 0)),
        ),
        scratch_shapes=[pltpu.VMEM((512, 1024), BF), pltpu.VMEM((1024, 512), BF)],
        compiler_params=pltpu.CompilerParams(vmem_limit_bytes=40 << 20),
        cost_estimate=pl.CostEstimate(flops=6 * 10**9, bytes_accessed=24 * 10**6, transcendentals=0),
        name="weight_grads",
    )(x, c, o, o, o)


def local(vision_tokens, image_counts, image_owner, gate_weight, up_weight, down_weight, out_grad):
    slots = vision_tokens.shape[0]
    row_count = lax.axis_size("row")
    col_count = lax.axis_size("col")
    token_total = out_grad.shape[0] * col_count
    owner, slot = token_place(image_counts, image_owner, token_total)
    owner_row = owner // col_count
    owner_col = owner % col_count
    core = lax.axis_index("row") % 2
    swap = [(i, i ^ 1) for i in range(row_count)]

    def other(a):
        return lax.ppermute(a, "row", swap)

    def halves(w, axis):
        mine = lax.dynamic_slice_in_dim(w, core * HALF, HALF, axis)
        theirs = lax.dynamic_slice_in_dim(w, (1 - core) * HALF, HALF, axis)
        return jnp.concatenate((mine, other(theirs)), axis=1 - axis)

    wg, wu, wd = halves(gate_weight, 1), halves(up_weight, 1), halves(down_weight, 0)
    received = lax.all_to_all(vision_tokens, "row", split_axis=1, concat_axis=0, tiled=True)
    pooled, cotangent = (
        lax.all_gather(received, "col", axis=0, tiled=True),
        lax.all_gather(out_grad, "col", axis=0, tiled=True),
    )
    pool_index = owner_col * (row_count * slots) + owner_row * slots + slot
    pool_index = pool_index.reshape(8, CHUNKS, 16).transpose(1, 0, 2).reshape(token_total)
    inputs = jnp.take(pooled, pool_index, axis=0)
    x2 = jnp.concatenate((inputs, other(inputs)), axis=1)
    c2 = jnp.concatenate((cotangent, other(cotangent)), axis=1).reshape(8, 128, 1024)
    layer_out, o = main_call(x2, c2, wg, wu, wd, down_weight)
    grad_gate, grad_up, grad_down = grads_call(inputs, cotangent.reshape(8, CHUNKS, 16, 512), o)
    return (layer_out, grad_gate, grad_up, grad_down)


def solution(mesh):
    in_specs = (
        P(("row", "col"), None),
        P(),
        P(),
        P("row", "col"),
        P("row", "col"),
        P("col", "row"),
        P("col", "row"),
    )
    out_specs = (P("col", "row"), P("row", "col"), P("row", "col"), P("col", "row"))
    return jax.shard_map(local, mesh=mesh, in_specs=in_specs, out_specs=out_specs, check_vma=False)
```

time: 551 us -> 256 us (0.46)
  waiting for transfers between devices: 471 us -> 82.9 us
  Pallas kernels: 0 us -> 108 us
  matrix products: 34.1 us -> 0 us
  other arithmetic: 5.16 us -> 13 us
  local copies, waits for them, and re-layouts: 11.4 us -> 17.7 us
    reduce_scatter x3 -> x0, waiting for transfers between devices: 301 us -> none  [the longest x1 164 us: local(): lax.psum_scatter(jnp.dot(block, both_weights, preferred_element_type=jnp....]
    pallas_call x0 -> x2, Pallas kernels: none -> 108 us  [the longest x1 99.2 us: main_call(): pl.pallas_call(main_kernel, out_shape=(jax.ShapeDtypeStruct((128, 512), B...]
    all_gather x2 -> x0, waiting for transfers between devices: 85.5 us -> none  [the longest x1 48.3 us: local(): pre_grads = lax.all_gather(grads_part, 'row', axis=0, tiled=True)]
    dot_general x5 -> x0, matrix products: 34.1 us -> none  [the longest x1 9.67 us: local(): jnp.dot(block, both_weights, preferred_element_type=jnp.float32)]
    concatenate x1 -> x5, other arithmetic: 0.8 us -> 12.3 us  [the longest x3 7.86 us: halves(): return jnp.concatenate((mine, other(theirs)), axis=1 - axis)]
    all_gather x1, waiting for transfers between devices: 35.7 us -> 28 us  [local(): lax.all_gather(out_grad, 'col', axis=0, tiled=True)]
    all_gather x1, waiting for transfers between devices: 48.2 us -> 54.2 us  [local(): lax.all_gather(received, 'col', axis=0, tiled=True)]
  transfers between devices with their start and end apart: 7 -> 7, of which waited for: 7 -> 2; matrix products, arithmetic and copies ran while one was open for 6% -> 10% of each run, Pallas kernels for 0% -> 0%
where the time goes in v1:
time: 256 us; the launch traced here: 254 us
  Pallas kernels  108 us (42%)
  waiting for transfers between devices  82.9 us (32%)
  local copies, waits for them, and re-layouts  17.7 us (7%)
  between operations  14.2 us (6%)
  blocking collectives  14.1 us (6%)
  other arithmetic  13 us (5%)
  starting transfers between devices  4.16 us (2%)
    pallas_call x1, Pallas kernels, main_call(): pl.pallas_call(main_kernel, out_shape=(jax.ShapeDtypeStruct((128, 512), B...  99.2 us
    all_gather x1, waiting for transfers between devices, local(): lax.all_gather(received, 'col', axis=0, tiled=True)  54.2 us
    all_gather x1, waiting for transfers between devices, local(): lax.all_gather(out_grad, 'col', axis=0, tiled=True)  28 us
    all_to_all x1, blocking collectives, local(): lax.all_to_all(vision_tokens, 'row', split_axis=1, concat_axis=0, tiled=T...  14.1 us
    pallas_call x1, Pallas kernels, grads_call(): pl.pallas_call(grads_kernel, grid=(1792 // width,), out_shape=(jax.ShapeD...  9.03 us
    concatenate x3, other arithmetic, halves(): return jnp.concatenate((mine, other(theirs)), axis=1 - axis)  7.86 us
    gather x1, local copies, waits for them, and re-layouts, local(): inputs = jnp.take(pooled, pool_index, axis=0)  5.85 us
    dynamic_slice x3, local copies, waits for them, and re-layouts, halves(): mine = lax.dynamic_slice_in_dim(w, core * HALF, HALF, axis)  5.21 us
  transfers between devices with their start and end apart: 7, of which 2 were waited for; matrix products, arithmetic and copies ran while one was open for 10% of the time, Pallas kernels for 0%

profile of v1, /device:TPU:1, one launch (start us, length us, event | category | flops | bytes accessed | tf_op | source)
XLA Modules:
  0.0 254.3 jit_solution(8904320770618966461)
XLA Ops:
  7.2 0.7 all-gather.5.cloned.1.call-update
  7.9 1.0 copy.25
  8.9 14.1 %all_to_all.19 = bf16[16,16,512]{2,0,1:T(8,128)(2,1)} all-to-all(bf16[16,16,512]{2,0,1:T(8,128)(2,1)S(1)} %bitcast.16), channel_id=1, replica_groups=mesh['row'=16,'col'=8] {'row'}, dimensions={1} | all-to-all | bytes 524288 | tf_op jit(solution)/shard_map/all_to_all | solution.py:367
  23.1 3.0 %constant_dynamic-slice_fusion.5 = (bf16[512,896]{1,0:T(8,128)(2,1)}, bf16[512,896]{1,0:T(8,128)(2,1)}) fusion(bf16[512,1792]{1,0:T(8,128)(2,1)} %param.10, s32[]{:T(128)S(6)} %select_n.65, s32[]{:T(128)S(6)} %select_n.66), kind=kLoop, calls=%fused_computation.50 | loop fusion | bytes 3670024 | tf_op jit(solution)/shard_map/dynamic_slice | solution.py:362
  26.1 0.4 collective-permute-start.2
  26.5 1.2 constant_dynamic-slice_fusion.3
  27.7 0.2 collective-permute-start.3
  27.9 1.0 constant_dynamic-slice_fusion.1
  28.9 0.4 collective-permute-start.4
  30.0 0.2 select_reduce_fusion.2
  30.8 28.0 %all-gather.5.cloned.1.call-done = bf16[1024,512]{1,0:T(8,128)(2,1)} async-done(((bf16[128,512]{1,0:T(8,128)(2,1)}), bf16[1024,512]{1,0:T(8,128)(2,1)}) %all-gather.5.cloned.1.call-update) | async-done | bytes 1048592 | tf_op jit(solution)/shard_map/all_gather | solution.py:370
  58.8 1.9 collective-permute-start.1
  60.7 54.2 %all-gather.3.cloned.1.call-done = bf16[2048,512]{1,0:T(8,128)(2,1)} async-done(((bf16[256,512]{1,0:T(8,128)(2,1)}), bf16[2048,512]{1,0:T(8,128)(2,1)}) %all-gather.3.cloned.1.call-update) | async-done | bytes 2097168 | tf_op jit(solution)/shard_map/all_gather | solution.py:369
  114.9 5.8 %gather_fusion = bf16[1024,512]{1,0:T(8,128)(2,1)S(1)} fusion(bf16[2048,512]{1,0:T(8,128)(2,1)} %all-gather.3.cloned.1.call-done, s32[1024]{0:T(1024)S(1)} %broadcast_clamp_fusion), kind=kCustom, calls=%fused_computation | custom fusion | bytes 2101248 | tf_op jit(solution)/shard_map/jit(_take)/gather | solution.py:374
  121.0 1.2 collective-permute-start
  122.2 2.6 %pad_maximum_fusion.2.wg_ref = bf16[1024,896]{1,0:T(8,128)(2,1)} fusion(bf16[512,896]{1,0:T(8,128)(2,1)} %collective-permute-done.2, bf16[512,896]{1,0:T(8,128)(2,1)S(1)} %copy-done.2), kind=kLoop, calls=%fused_computation.3 | loop fusion | flops 3670016 | bytes 3670016 | tf_op jit(solution)/shard_map/concatenate | solution.py:364
  124.7 2.6 %pad_maximum_fusion.3.wu_ref = bf16[1024,896]{1,0:T(8,128)(2,1)} fusion(bf16[512,896]{1,0:T(8,128)(2,1)} %collective-permute-done.3, bf16[512,896]{1,0:T(8,128)(2,1)S(1)} %get-tuple-element.20), kind=kLoop, calls=%fused_computation.4 | loop fusion | flops 3670016 | bytes 3670016 | tf_op jit(solution)/shard_map/concatenate | solution.py:364
  127.3 2.7 %pad_maximum_fusion.4.wd_ref = bf16[896,1024]{1,0:T(8,128)(2,1)} fusion(bf16[896,512]{1,0:T(8,128)(2,1)} %collective-permute-done.4, bf16[896,512]{1,0:T(8,128)(2,1)S(1)} %get-tuple-element.18), kind=kLoop, calls=%fused_computation.5 | loop fusion | flops 3670016 | bytes 3670016 | tf_op jit(solution)/shard_map/concatenate | solution.py:364
  130.0 2.8 %pad_maximum_fusion.1 = bf16[1024,1024]{1,0:T(8,128)(2,1)} fusion(bf16[1024,512]{1,0:T(8,128)(2,1)} %collective-permute-done.1, bf16[1024,512]{1,0:T(8,128)(2,1)S(1)} %copy-done.1), kind=kLoop, calls=%fused_computation.2 | loop fusion | flops 4194304 | bytes 4194304 | tf_op jit(solution)/shard_map/concatenate | solution.py:376
  132.8 1.6 pad_maximum_fusion.x_ref
  134.5 99.2 %row_sums.1 = (bf16[128,512]{1,0:T(8,128)(2,1)}, bf16[8,4,2,3,16,1792]{5,4,3,2,1,0:T(8,128)(2,1)}) custom-call(bf16[1024,1024]{1,0:T(8,128)(2,1)} %pad_maximum_fusion.x_ref, bf16[8,128,1024]{2,1,0:T(8,128)(2,1)} %bitcast.14, bf16[1024,896]{1,0:T(8,128)(2,1)} %pad_maximum_fusion.2.wg_ref, bf16[1024,896]{1,0:T(8,128)(2,1)} %pad_maximum_fusion.3.wu_ref, ...), custom_call_target="tpu_custom_call" | custom-call | flops 8000000000 | bytes 30000000 | tf_op jit(solution)/shard_map/row_sums/pallas_call | solution.py:280
  233.7 4.1 %copy-done = bf16[8,4,2,3,16,1792]{5,4,3,2,1,0:T(8,128)(2,1)S(1)} copy-done((bf16[8,4,2,3,16,1792]{5,4,3,2,1,0:T(8,128)(2,1)S(1)}, bf16[8,4,2,3,16,1792]{5,4,3,2,1,0:T(8,128)(2,1)}, u32[]{:S(2)}) %copy-start) | copy-done | bytes 11010072
  237.8 9.0 %weight_grads.1 = (f32[512,1792]{1,0:T(8,128)}, f32[512,1792]{1,0:T(8,128)}, f32[1792,512]{1,0:T(8,128)}) custom-call(bf16[1024,512]{1,0:T(8,128)(2,1)S(1)} %broadcast_select_fusion.x_ref, bf16[8,8,16,512]{3,2,1,0:T(8,128)(2,1)S(1)} %bitcast.13, bf16[8,4,2,3,16,1792]{5,4,3,2,1,0:T(8,128)(2,1)S(1)} %copy-done, bf16[8,4,2,3,16,1792]{5,4,3,2,1,0:T(8,128)(2,1)S(1)} %copy-done, ...), custom_call_target="tpu_custom_call" | custom-call | flops 6000000000 | bytes 24000000 | tf_op jit(solution)/shard_map/weight_grads/pallas_call | solution.py:322
  246.8 0.7 copy.27
  (42 shorter events, 1.5 us)
Async XLA Ops:
  7.2 51.7 %all-gather.5.cloned.1.call-start = ((), (), s32[]{:S(2)}) async-start(), calls=%async_computation.2 | async-start | bytes 1179648 | tf_op jit(solution)/shard_map/all_gather | solution.py:370
  7.9 107.0 %all-gather.3.cloned.1.call-start = ((), (), s32[]{:S(2)}) async-start(), calls=%async_computation.1 | async-start | bytes 2359296 | tf_op jit(solution)/shard_map/all_gather | solution.py:369
  23.0 3.4 %copy-start.3 = (bf16[512,1792]{1,0:T(8,128)(2,1)S(1)}, bf16[512,1792]{1,0:T(8,128)(2,1)}, u32[]{:S(2)}) copy-start(bf16[512,1792]{1,0:T(8,128)(2,1)} %param.11) | copy-start | bytes 5505028
  26.1 1.8 copy-start.4
  26.1 96.1 %collective-permute-start.2 = (bf16[512,896]{1,0:T(8,128)(2,1)}, bf16[512,896]{1,0:T(8,128)(2,1)}, u32[]{:S(2)}, u32[]{:S(2)}) collective-permute-start(bf16[512,896]{1,0:T(8,128)(2,1)} %get-tuple-element.23), channel_id=1, source_target_pairs={{0,8},{8,0},{16,24},{24,16},{32,40},{40,32},{48,56},{56,48},{64,72... | collective-permute-start | bytes 2752520 | tf_op jit(solution)/shard_map/ppermute | solution.py:359
  27.7 1.7 copy-start.7
  27.7 2.0 copy-start.6
  27.7 97.0 %collective-permute-start.3 = (bf16[512,896]{1,0:T(8,128)(2,1)}, bf16[512,896]{1,0:T(8,128)(2,1)}, u32[]{:S(2)}, u32[]{:S(2)}) collective-permute-start(bf16[512,896]{1,0:T(8,128)(2,1)} %get-tuple-element.21), channel_id=1, source_target_pairs={{0,8},{8,0},{16,24},{24,16},{32,40},{40,32},{48,56},{56,48},{64,72... | collective-permute-start | bytes 2752520 | tf_op jit(solution)/shard_map/ppermute | solution.py:359
  28.9 98.4 %collective-permute-start.4 = (bf16[896,512]{1,0:T(8,128)(2,1)}, bf16[896,512]{1,0:T(8,128)(2,1)}, u32[]{:S(2)}, u32[]{:S(2)}) collective-permute-start(bf16[896,512]{1,0:T(8,128)(2,1)} %get-tuple-element.19), channel_id=1, source_target_pairs={{0,8},{8,0},{16,24},{24,16},{32,40},{40,32},{48,56},{56,48},{64,72... | collective-permute-start | bytes 2752520 | tf_op jit(solution)/shard_map/ppermute | solution.py:359
  58.8 71.2 %collective-permute-start.1 = (bf16[1024,512]{1,0:T(8,128)(2,1)}, bf16[1024,512]{1,0:T(8,128)(2,1)}, u32[]{:S(2)}, u32[]{:S(2)}) collective-permute-start(bf16[1024,512]{1,0:T(8,128)(2,1)} %all-gather.5.cloned.1.call-done), channel_id=1, source_target_pairs={{0,8},{8,0},{16,24},{24,16},{32,40},{40,32},{48,56},{56,48},{64,72... | collective-permute-start | bytes 3145736 | tf_op jit(solution)/shard_map/ppermute | solution.py:359
  120.8 1.4 copy-start.2
  121.0 11.9 %collective-permute-start = (bf16[1024,512]{1,0:T(8,128)(2,1)S(1)}, bf16[1024,512]{1,0:T(8,128)(2,1)S(1)}, u32[]{:S(2)}, u32[]{:S(2)}) collective-permute-start(bf16[1024,512]{1,0:T(8,128)(2,1)S(1)} %broadcast_select_fusion.x_ref), channel_id=1, source_target_pairs={{0,8},{8,0},{16,24},{24,16},{32,40},{40,32},{48,56},{56,48},{64,72... | collective-permute-start | bytes 3145736 | tf_op jit(solution)/shard_map/ppermute | solution.py:359
  127.3 2.7 %copy-start.1 = (bf16[1024,512]{1,0:T(8,128)(2,1)S(1)}, bf16[1024,512]{1,0:T(8,128)(2,1)}, u32[]{:S(2)}) copy-start(bf16[1024,512]{1,0:T(8,128)(2,1)} %all-gather.5.cloned.1.call-done) | copy-start | bytes 3145732
  233.7 4.1 %copy-start = (bf16[8,4,2,3,16,1792]{5,4,3,2,1,0:T(8,128)(2,1)S(1)}, bf16[8,4,2,3,16,1792]{5,4,3,2,1,0:T(8,128)(2,1)}, u32[]{:S(2)}) copy-start(bf16[8,4,2,3,16,1792]{5,4,3,2,1,0:T(8,128)(2,1)} %get-tuple-element.10.h_ref.gg_ref.ug_ref) | copy-start | bytes 33030148
  237.8 9.0 %copy-start.5 = (bf16[128,512]{1,0:T(8,128)(2,1)S(1)}, bf16[128,512]{1,0:T(8,128)(2,1)}, u32[]{:S(2)}) copy-start(bf16[128,512]{1,0:T(8,128)(2,1)} %get-tuple-element.28) | copy-start | bytes 393220
Sparse Core Ops, SparseCore 0:
  10.4 48.4 all-gather.4
  61.2 53.6 all-gather.2

commit v2 on v0

v2 whole, which is shorter than its diff:
```python
import functools
import jax
import jax.numpy as jnp
from jax import lax
from jax.experimental import pallas as pl
from jax.experimental.pallas import tpu as pltpu
from jax.sharding import PartitionSpec as P

BF = jnp.bfloat16
F32 = jnp.float32
MESH = pl.DeviceIdType.MESH

CHUNKS = 8
HALF = 896
XW = 512
YW = HALF - XW

XD, XR, X2, XY, YY, YD, YR, Y2 = range(8)
HG = 8
AXY, AXP, AXM, AXF, AYP, AYM, AYF, AYY, CORE, XIN, CIN, LOZ = range(16, 28)
KINDS = 28
CP, CM, CY, CF1, CF2, DP, DM, DF1, DF2 = range(9)
VY, VP, VM, WP, WM, VF1, VF2, VH, WF1, WF2 = range(9, 19)
WG, WU, WD, LOY = range(19, 23)
ONCE = 23
FIRST = 7
VR = 12

def token_place(image_counts, image_owner, total):
    position = jnp.arange(total, dtype=jnp.int32)
    ends = jnp.cumsum(image_counts)
    starts = ends - image_counts
    member = ((position[:, None] >= starts[None, :]) & (position[:, None] < ends[None, :])).astype(
        jnp.int32
    )
    count = jnp.sum(member * image_counts[None, :], axis=1)
    begin = jnp.sum(member * starts[None, :], axis=1)
    owner_first = jnp.sum(member * image_owner[0::2][None, :], axis=1)
    owner_second = jnp.sum(member * image_owner[1::2][None, :], axis=1)
    first = (count + 1) // 2
    within = position - begin
    second = (within >= first).astype(jnp.int32)
    slot = within - second * first
    owner = jnp.where(second > 0, owner_second, owner_first)
    return (owner, slot)


def rem(a, n):
    return lax.rem(a, n)


class RowSum:
    def __init__(self, base, refs):
        self.base = base
        (self.px, self.py, self.sxd, self.sxr, self.sx2, self.sxy, self.syy, self.syd, self.syr,
         self.sy2, self.rxd, self.rxr, self.rx2, self.rxy, self.ryy, self.ryd, self.ryr, self.ry2) = refs


def main_kernel(
    v_ref, pos_ref, og_ref, gate_hbm, up_hbm, down_hbm,
    out_ref, o_ref, xo_ref, co_ref,
    act, pool, xin, c2, wg, wu, wd, wdo,
    hfx, hfy, lo, rz, zs, rh,
    *rest,
):
    gu, hg = RowSum(0, rest[:18]), RowSum(HG, rest[18:36])
    ssem, rsem, ssem1, rsem1, sa, ra, osem, lsem = rest[36:]
    row = lax.axis_index("row")
    col = lax.axis_index("col")
    x, y, k = row // 4, rem(row // 2, 2), rem(row, 2)
    yh, z = col // 4, rem(col, 4)
    yo, ko, ho = 1 - y, 1 - k, 1 - yh
    far = rem(x + 2, 4)
    zp, zm, zf = rem(z + 1, 4), rem(z + 3, 4), rem(z + 2, 4)

    def at_row(xx, yy, kk):
        return {"row": xx * 4 + yy * 2 + kk}

    def at_col(hh, zz):
        return {"col": hh * 4 + zz}

    y_dev, core_dev = at_row(x, yo, k), at_row(x, y, ko)
    up_dev, down_dev, hi_dev = at_col(yh, zp), at_col(yh, zm), at_col(ho, z)
    barrier = pltpu.get_barrier_semaphore()

    def greet(i, carry):
        pl.semaphore_signal(barrier, inc=1, device_id={"row": rem(row + i, 16)}, device_id_type=MESH)
        return carry

    lax.fori_loop(1, 16, greet, 0)
    for dev in (up_dev, down_dev, at_col(yh, zf), hi_dev):
        pl.semaphore_signal(barrier, inc=1, device_id=dev, device_id_type=MESH)

    mine = pl.ds(pl.multiple_of(k * HALF, 128), HALF)
    theirs = pl.ds(pl.multiple_of(ko * HALF, 128), HALF)
    here = [
        pltpu.make_async_copy(down_hbm.at[mine, :], wd.at[:, 0:512], lsem.at[0]),
        pltpu.make_async_copy(gate_hbm.at[:, mine], wg.at[0:512, :], lsem.at[1]),
        pltpu.make_async_copy(up_hbm.at[:, mine], wu.at[0:512, :], lsem.at[2]),
        pltpu.make_async_copy(down_hbm, wdo, lsem.at[3]),
    ]
    here[0].start()
    c2[col, :, 0:512] = og_ref[...]
    pool[yh, z, row] = v_ref[:, pl.ds(pl.multiple_of(row * 512, 512), 512)]
    pl.semaphore_wait(barrier, 19)

    cx = pl.ds(pl.multiple_of(k * HALF, 128), XW)
    cy = pl.ds(pl.multiple_of(k * HALF + XW, 128), YW)

    def copy(kind, t, src, dst, dev):
        return pltpu.make_async_remote_copy(
            src_ref=src, dst_ref=dst, send_sem=ssem.at[kind, t], recv_sem=rsem.at[kind, t],
            device_id=dev, device_id_type=MESH,
        )

    def once(kind, src, dst, dev):
        return pltpu.make_async_remote_copy(
            src_ref=src, dst_ref=dst, send_sem=ssem1.at[kind], recv_sem=rsem1.at[kind],
            device_id=dev, device_id_type=MESH,
        )

    def same(ref):
        return ref, ref

    def cblk(hh, zz, lo_=0, n=128):
        return c2.at[hh * 4 + zz, lo_:lo_ + n, 0:512]

    single = {
        WD: lambda: (down_hbm.at[theirs, :], wd.at[:, 512:1024], core_dev, wd.at[:, 512:1024]),
        WG: lambda: (gate_hbm.at[:, theirs], wg.at[512:1024, :], core_dev, wg.at[512:1024, :]),
        WU: lambda: (up_hbm.at[:, theirs], wu.at[512:1024, :], core_dev, wu.at[512:1024, :]),
        CP: lambda: (*same(cblk(yh, z)), up_dev, cblk(yh, zm)),
        CM: lambda: (*same(cblk(yh, z)), down_dev, cblk(yh, zp)),
        CY: lambda: (*same(cblk(yh, z)), hi_dev, cblk(ho, z)),
        CF1: lambda: (*same(cblk(yh, zm, 0, 64)), up_dev, cblk(yh, zf, 0, 64)),
        CF2: lambda: (*same(cblk(yh, zp, 64, 64)), down_dev, cblk(yh, zf, 64, 64)),
        DP: lambda: (*same(cblk(ho, z)), up_dev, cblk(ho, zm)),
        DM: lambda: (*same(cblk(ho, z)), down_dev, cblk(ho, zp)),
        DF1: lambda: (*same(cblk(ho, zm, 0, 64)), up_dev, cblk(ho, zf, 0, 64)),
        DF2: lambda: (*same(cblk(ho, zp, 64, 64)), down_dev, cblk(ho, zf, 64, 64)),
        VY: lambda: (*same(pool.at[yh, z, 0:VR]), hi_dev, pool.at[ho, z, 0:VR]),
        VP: lambda: (*same(pool.at[yh, z, VR:16]), up_dev, pool.at[yh, zm, VR:16]),
        VM: lambda: (*same(pool.at[yh, z, VR:16]), down_dev, pool.at[yh, zp, VR:16]),
        VF1: lambda: (*same(pool.at[yh, zm, VR:VR + 2]), up_dev, pool.at[yh, zf, VR:VR + 2]),
        VF2: lambda: (*same(pool.at[yh, zp, VR + 2:16]), down_dev, pool.at[yh, zf, VR + 2:16]),
        VH: lambda: (*same(pool.at[yh, :, VR:16]), hi_dev, pool.at[ho, :, VR:16]),
        WP: lambda: (*same(pool.at[:, z, 0:VR]), up_dev, pool.at[:, zm, 0:VR]),
        WM: lambda: (*same(pool.at[:, z, 0:VR]), down_dev, pool.at[:, zp, 0:VR]),
        WF1: lambda: (*same(pool.at[:, zm, 0:VR // 2]), up_dev, pool.at[:, zf, 0:VR // 2]),
        WF2: lambda: (*same(pool.at[:, zp, VR // 2:VR]), down_dev, pool.at[:, zf, VR // 2:VR]),
        LOY: lambda: (zs, rh, hi_dev, rh),
    }

    def start1(*kinds):
        for kind in kinds:
            src, dst, dev, _ = single[kind]()
            once(kind, src, dst, dev).start()

    def arrive1(*kinds):
        for kind in kinds:
            place = single[kind]()[3]
            once(kind, place, place, y_dev).wait_recv()

    def sides(t):
        s = 1 - 2 * rem(t, 2)
        return rem(x + s + 4, 4), rem(x - s + 4, 4)

    def tok(t):
        return rem(yh + 1 + t // 4, 2) * 4 + rem(z + 1 + rem(t, 4), 4)

    def tokh(u):
        w = rem(u, 4)
        return rem(yh + u // 4, 2) * 4 + rem(z + w + (w // 2) * (5 - 2 * w), 4)

    def table(kind, t):
        ahead, back = sides(t)
        to_ahead, to_back = at_row(ahead, y, k), at_row(back, y, k)
        if kind < 16:
            r = gu if kind < HG else hg
            src, dst, dev = {
                XD: lambda: (r.sxd, r.rxd, to_ahead), XR: lambda: (r.sxr, r.rxr, to_back),
                X2: lambda: (r.sx2, r.rx2, to_back), XY: lambda: (r.sxy, r.rxy, y_dev),
                YY: lambda: (r.syy, r.ryy, y_dev), YD: lambda: (r.syd, r.ryd, to_ahead),
                YR: lambda: (r.syr, r.ryr, to_back), Y2: lambda: (r.sy2, r.ry2, to_back),
            }[kind % HG]()
            return src.at[t], dst.at[t], dev, dst.at[t]
        if kind == CIN:
            c = tokh(t)
            return c2.at[c, :, 0:512], c2.at[c, :, 512:1024], core_dev, c2.at[c, :, 512:1024]
        c = tok(t)
        return {
            AXY: lambda: (*same(act.at[c, x, y, :, :, cx]), y_dev, act.at[c, x, yo, :, :, cx]),
            AXP: lambda: (*same(act.at[c, x, :, :, :, cx]), to_ahead, act.at[c, back, :, :, :, cx]),
            AXM: lambda: (*same(act.at[c, x, :, :, :, cx]), to_back, act.at[c, ahead, :, :, :, cx]),
            AXF: lambda: (*same(act.at[c, back, :, :, :, cx]), to_ahead, act.at[c, far, :, :, :, cx]),
            AYP: lambda: (*same(act.at[c, x, y, :, :, cy]), to_ahead, act.at[c, back, y, :, :, cy]),
            AYM: lambda: (*same(act.at[c, x, y, :, :, cy]), to_back, act.at[c, ahead, y, :, :, cy]),
            AYF: lambda: (*same(act.at[c, back, y, :, :, cy]), to_ahead, act.at[c, far, y, :, :, cy]),
            AYY: lambda: (*same(act.at[c, :, y, :, :, cy]), y_dev, act.at[c, :, yo, :, :, cy]),
            CORE: lambda: (*same(act.at[c, :, :, :, :, mine]), core_dev, act.at[c, :, :, :, :, theirs]),
            XIN: lambda: (xin.at[c, :, 0:512], xin.at[c, :, 512:1024], core_dev, xin.at[c, :, 512:1024]),
            LOZ: lambda: (lo.at[t], rz.at[t], at_col(yh, rem(c, 4)), rz.at[t]),
        }[kind]()

    def start(t, *kinds):
        for kind in kinds:
            src, dst, dev, _ = table(kind, t)
            copy(kind, t, src, dst, dev).start()

    def arrive(t, *kinds):
        for kind in kinds:
            place = table(kind, t)[3]
            copy(kind, t, place, place, y_dev).wait_recv()

    def r0(r, t, parts):
        b = rem(t, 4)
        ahead, _ = sides(t)
        for m, g in enumerate(parts):
            r.px[b, :, m] = g[:, :XW].reshape(4, 32, XW)
            gy = g[:, XW:].reshape(4, 2, 16, YW)
            for yy in range(2):
                r.py[b, yy, :, m] = gy[:, yy]
        r.sxd[t] = r.px[b, ahead].astype(BF)
        r.sxr[t] = r.px[b, far].astype(BF)
        start(t, r.base + XD, r.base + XR)
        r.syy[t] = r.py[b, yo].astype(BF)
        start(t, r.base + YY)

    def r1(r, t):
        b = rem(t, 4)
        ahead, back = sides(t)
        arrive(t, r.base + XR)
        r.sx2[t] = (r.px[b, back] + r.rxr[t].astype(F32)).astype(BF)
        start(t, r.base + X2)
        arrive(t, r.base + YY)
        r.py[b, y] = r.py[b, y] + r.ryy[t].astype(F32)
        r.syd[t] = r.py[b, y, ahead].astype(BF)
        r.syr[t] = r.py[b, y, far].astype(BF)
        start(t, r.base + YD, r.base + YR)

    def r2(r, t):
        b = rem(t, 4)
        _, back = sides(t)
        arrive(t, r.base + XD, r.base + X2)
        r.px[b, x] = r.px[b, x] + r.rxd[t].astype(F32) + r.rx2[t].astype(F32)
        r.sxy[t] = r.px[b, x, :, pl.ds(pl.multiple_of(yo * 16, 16), 16), :].astype(BF)
        start(t, r.base + XY)
        arrive(t, r.base + YR)
        r.sy2[t] = (r.py[b, y, back] + r.ryr[t].astype(F32)).astype(BF)
        start(t, r.base + Y2)

    def r3x(r, t):
        b = rem(t, 4)
        arrive(t, r.base + XY)
        return r.px[b, x, :, pl.ds(pl.multiple_of(y * 16, 16), 16), :] + r.rxy[t].astype(F32)

    def r3y(r, t):
        b = rem(t, 4)
        arrive(t, r.base + YD, r.base + Y2)
        return r.py[b, y, x] + r.ryd[t].astype(F32) + r.ry2[t].astype(F32)

    def hx(u):
        start(u, CIN)

    def h0(u):
        arrive(u, CIN)
        r0(hg, u, [lax.dot_general(c2[tokh(u)], wd[...], (((1,), (1,)), ((), ())), preferred_element_type=F32)])

    def h3(u):
        c = tokh(u)
        hfx[c] = r3x(hg, u)[0]
        hfy[c] = r3y(hg, u)[0]

    def p0(t):
        c = tok(t)
        spot = pos_ref[pl.ds(pl.multiple_of(c * 128, 128), 128), :]
        pick = jnp.where(lax.broadcasted_iota(jnp.int32, (128, 2048), 1) == spot, 1.0, 0.0).astype(BF)
        own = jnp.dot(pick, pool[...].reshape(2048, 512), preferred_element_type=F32)
        xin[c, :, 0:512] = own.astype(BF)
        start(t, XIN)
        pltpu.make_async_copy(xin.at[c, :, 0:512], xo_ref.at[c], osem.at[1, t]).start()

    def s0(t):
        arrive(t, XIN)
        x_t = xin[tok(t)]
        r0(gu, t, [jnp.dot(x_t, w[...], preferred_element_type=F32) for w in (wg, wu)])

    def activate(c, full, hgrad, cols):
        gate, up = full[0], full[1]
        sigma = jax.nn.sigmoid(gate)
        act[c, x, y, 0, :, cols] = (gate * sigma * up).astype(BF)
        act[c, x, y, 1, :, cols] = (hgrad * up * sigma * (1.0 + gate * (1.0 - sigma))).astype(BF)
        act[c, x, y, 2, :, cols] = (hgrad * gate * sigma).astype(BF)

    def s3(t):
        c = tok(t)
        activate(c, r3x(gu, t), hfx[c], cx)
        start(t, AXY)
        activate(c, r3y(gu, t), hfy[c], cy)
        start(t, AYP, AYM)

    def s4(t):
        arrive(t, AXY)
        start(t, AXP, AXM)
        arrive(t, AYP)
        start(t, AYF)
        arrive(t, AYM)

    def s5(t):
        arrive(t, AXP)
        start(t, AXF)
        arrive(t, AXM)
        arrive(t, AYF)
        start(t, AYY)

    def s6(t):
        arrive(t, AXF, AYY)
        start(t, CORE)

    def s7(t):
        c = tok(t)
        arrive(t, CORE)
        pltpu.make_async_copy(act.at[c], o_ref.at[c], osem.at[0, t]).start()
        hidden = act[c, :, :, 0].reshape(128, 2 * HALF)
        lo[t] = jnp.dot(hidden, wdo[...], preferred_element_type=F32)

        @pl.when(rem(t, 4) < 3)
        def _():
            start(t, LOZ)

        @pl.when(t == 7)
        def _():
            arrive(4, LOZ)
            arrive(5, LOZ)
            arrive(6, LOZ)
            arrive1(LOY)
            out_ref[...] = (lo[7] + rz[4] + rz[5] + rz[6] + rh[...]).astype(BF)

    def s8(t):
        @pl.when(t == 3)
        def _():
            arrive(0, LOZ)
            arrive(1, LOZ)
            arrive(2, LOZ)
            zs[...] = lo[3] + rz[0] + rz[1] + rz[2]
            start1(LOY)

    def spread(i, carry):
        to = rem(row + i, 16)
        pltpu.make_async_remote_copy(
            src_ref=v_ref.at[:, pl.ds(pl.multiple_of(to * 512, 512), 512)],
            dst_ref=pool.at[yh, z, row],
            send_sem=sa.at[i], recv_sem=ra.at[i], device_id={"row": to}, device_id_type=MESH,
        ).start()
        return carry

    def spread_in(i, carry):
        place = pool.at[yh, z, rem(row + 16 - i, 16)]
        pltpu.make_async_remote_copy(
            src_ref=place, dst_ref=place, send_sem=sa.at[i], recv_sem=ra.at[i],
            device_id=y_dev, device_id_type=MESH,
        ).wait_recv()
        return carry

    def spread_out(i, carry):
        place = v_ref.at[:, 0:512]
        pltpu.make_async_remote_copy(
            src_ref=place, dst_ref=pool.at[yh, z, row], send_sem=sa.at[i], recv_sem=ra.at[i],
            device_id=y_dev, device_id_type=MESH,
        ).wait_send()
        return carry

    lax.fori_loop(1, 16, spread, 0)
    start1(WD, CP, CM, CY)
    for c in here[1:]:
        c.start()

    def c_1():
        arrive1(CP)
        start1(CF1)
        arrive1(CM)
        start1(CF2)
        arrive1(CY)
        start1(DP, DM)

    def c_3():
        arrive1(CF1, CF2, DP)
        start1(DF1)
        arrive1(DM)
        start1(DF2)

    def c_7():
        arrive1(DF1, DF2)
        pltpu.make_async_copy(c2.at[:, :, 0:512], co_ref, lsem.at[4]).start()

    def v_0():
        lax.fori_loop(1, 16, spread_in, 0)
        start1(VY, VP, VM)

    def v_2():
        arrive1(VY)
        start1(WP, WM)
        arrive1(VP)
        start1(VF1)
        arrive1(VM)
        start1(VF2)

    def v_4():
        arrive1(VF1, VF2)
        start1(VH)
        arrive1(WP)
        start1(WF1)
        arrive1(WM)
        start1(WF2)

    def v_6():
        arrive1(WF1, WF2, VH)

    def w_1():
        here[0].wait()
        arrive1(WD)
        start1(WG, WU)

    def w_8():
        here[1].wait()
        here[2].wait()
        here[3].wait()
        arrive1(WG, WU)

    def each(n, lag, stage):
        t = n - lag

        @pl.when((t >= 0) & (t < CHUNKS))
        def _():
            stage(t)

    def at(n, when, stage):
        @pl.when(n == when)
        def _():
            stage()

    def step(n, carry):
        at(n, 1, c_1)
        at(n, 3, c_3)
        at(n, 7, c_7)
        at(n, 1, w_1)
        for lag, stage in enumerate(
            [hx, h0, lambda u: r1(hg, u), lambda u: r2(hg, u), h3]
        ):
            each(n, lag, stage)
        at(n, 0, v_0)
        at(n, 2, v_2)
        at(n, 4, v_4)
        at(n, 6, v_6)
        at(n, FIRST + 1, w_8)
        for lag, stage in enumerate(
            [p0, s0, lambda t: r1(gu, t), lambda t: r2(gu, t), s3, s4, s5, s6, s7, s8]
        ):
            each(n, FIRST + lag, stage)
        return carry

    lax.fori_loop(0, FIRST + CHUNKS + 9, step, 0)

    def sent(kind, t):
        src, dst, dev, _ = table(kind, t)
        copy(kind, t, src, dst, dev).wait_send()

    def finish(t, carry):
        for kind in range(KINDS):
            if kind != LOZ:
                sent(kind, t)

        @pl.when(rem(t, 4) < 3)
        def _():
            sent(LOZ, t)

        c = tok(t)
        pltpu.make_async_copy(act.at[c], o_ref.at[c], osem.at[0, t]).wait()
        pltpu.make_async_copy(xin.at[c, :, 0:512], xo_ref.at[c], osem.at[1, t]).wait()
        return carry

    lax.fori_loop(0, CHUNKS, finish, 0)
    lax.fori_loop(1, 16, spread_out, 0)
    for kind in range(ONCE):
        src, dst, dev, _ = single[kind]()
        once(kind, src, dst, dev).wait_send()
    pltpu.make_async_copy(c2.at[:, :, 0:512], co_ref, lsem.at[4]).wait()


def main_call(v, pos, og, gate, up, down):
    n = CHUNKS
    vm = lambda *s: pltpu.VMEM(s, BF)
    vf = lambda *s: pltpu.VMEM(s, F32)

    def row_sum(mats):
        xb, xq, yb = (n, mats, 32, XW), (n, mats, 16, XW), (n, mats, 16, YW)
        moves = [vm(*xb), vm(*xb), vm(*xb), vm(*xq), vm(n, 4, mats, 16, YW), vm(*yb), vm(*yb), vm(*yb)]
        return [vf(4, 4, mats, 32, XW), vf(4, 2, 4, mats, 16, YW), *moves, *moves]

    dma = pltpu.SemaphoreType.DMA
    vmem = pl.BlockSpec(memory_space=pltpu.VMEM)
    hbm = pl.BlockSpec(memory_space=pl.ANY)
    return pl.pallas_call(
        main_kernel,
        out_shape=(
            jax.ShapeDtypeStruct((128, 512), BF),
            jax.ShapeDtypeStruct((n, 4, 2, 3, 16, 2 * HALF), BF),
            jax.ShapeDtypeStruct((n, 128, 512), BF),
            jax.ShapeDtypeStruct((n, 128, 512), BF),
        ),
        in_specs=[vmem, vmem, vmem, hbm, hbm, hbm],
        out_specs=(vmem, hbm, hbm, hbm),
        scratch_shapes=[
            vm(n, 4, 2, 3, 16, 2 * HALF), vm(2, 4, 16, 16, 512), vm(n, 128, 1024), vm(n, 128, 1024),
            vm(1024, HALF), vm(1024, HALF), vm(HALF, 1024), vm(2 * HALF, 512),
            vf(n, 16, XW), vf(n, 16, YW),
            vf(n, 128, 512), vf(n, 128, 512), vf(128, 512), vf(128, 512),
            *row_sum(2), *row_sum(1),
            dma((KINDS, n)), dma((KINDS, n)), dma((ONCE,)), dma((ONCE,)), dma((16,)), dma((16,)),
            dma((2, n)), dma((5,)),
        ],
        compiler_params=pltpu.CompilerParams(
            collective_id=0, has_side_effects=True, vmem_limit_bytes=60 << 20
        ),
        cost_estimate=pl.CostEstimate(flops=10**10, bytes_accessed=30 * 10**6, transcendentals=0),
        name="row_sums",
    )(v, pos, og, gate, up, down)


def grads_kernel(x_ref, c_ref, h_ref, gg_ref, ug_ref, gate_ref, up_ref, down_ref, xt):
    @pl.when(pl.program_id(0) == 0)
    def _():
        xt[...] = x_ref[...].reshape(1024, 512).T

    width = h_ref.shape[-1]
    gate_ref[...] = jnp.dot(xt[...], gg_ref[...].reshape(1024, width), preferred_element_type=F32)
    up_ref[...] = jnp.dot(xt[...], ug_ref[...].reshape(1024, width), preferred_element_type=F32)
    down_ref[...] = lax.dot_general(
        h_ref[...].reshape(1024, width), c_ref[...].reshape(1024, 512), (((0,), (0,)), ((), ())), preferred_element_type=F32
    )


def grads_call(x, c, o):
    width = 256
    n = CHUNKS
    part = lambda m: pl.BlockSpec((n, 4, 2, 1, 16, width), lambda j: (0, 0, 0, m, 0, j))
    return pl.pallas_call(
        grads_kernel,
        grid=(1792 // width,),
        out_shape=(
            jax.ShapeDtypeStruct((512, 1792), F32),
            jax.ShapeDtypeStruct((512, 1792), F32),
            jax.ShapeDtypeStruct((1792, 512), F32),
        ),
        in_specs=[
            pl.BlockSpec((n, 128, 512), lambda j: (0, 0, 0)),
            pl.BlockSpec((n, 128, 512), lambda j: (0, 0, 0)),
            part(0), part(1), part(2),
        ],
        out_specs=(
            pl.BlockSpec((512, width), lambda j: (0, j)),
            pl.BlockSpec((512, width), lambda j: (0, j)),
            pl.BlockSpec((width, 512), lambda j: (j, 0)),
        ),
        scratch_shapes=[pltpu.VMEM((512, 1024), BF)],
        compiler_params=pltpu.CompilerParams(vmem_limit_bytes=60 << 20),
        cost_estimate=pl.CostEstimate(flops=6 * 10**9, bytes_accessed=24 * 10**6, transcendentals=0),
        name="weight_grads",
    )(x, c, o, o, o)


def local(vision_tokens, image_counts, image_owner, gate_weight, up_weight, down_weight, out_grad):
    slots = vision_tokens.shape[0]
    row_count = lax.axis_size("row")
    col_count = lax.axis_size("col")
    token_total = out_grad.shape[0] * col_count
    owner, slot = token_place(image_counts, image_owner, token_total)
    owner_row = owner // col_count
    owner_col = owner % col_count
    pool_index = owner_col * (row_count * slots) + owner_row * slots + slot
    layer_out, o, x, c = main_call(
        vision_tokens, pool_index[:, None], out_grad, gate_weight, up_weight, down_weight
    )
    grad_gate, grad_up, grad_down = grads_call(x, c, o)
    return (layer_out, grad_gate, grad_up, grad_down)


def solution(mesh):
    in_specs = (
        P(("row", "col"), None),
        P(),
        P(),
        P("row", "col"),
        P("row", "col"),
        P("col", "row"),
        P("col", "row"),
    )
    out_specs = (P("col", "row"), P("row", "col"), P("row", "col"), P("col", "row"))
    return jax.shard_map(local, mesh=mesh, in_specs=in_specs, out_specs=out_specs, check_vma=False)
```

time: 551 us -> 152 us (0.28)
  waiting for transfers between devices: 471 us -> 0 us
  Pallas kernels: 0 us -> 143 us
  matrix products: 34.1 us -> 0 us
  blocking collectives: 14.1 us -> 0 us
  between operations: 14.2 us -> 0.7 us
  local copies, waits for them, and re-layouts: 11.4 us -> 3.92 us
    reduce_scatter x3 -> x0, waiting for transfers between devices: 301 us -> none  [the longest x1 164 us: local(): lax.psum_scatter(jnp.dot(block, both_weights, preferred_element_type=jnp....]
    all_gather x4 -> x0, waiting for transfers between devices: 169 us -> none  [the longest x1 48.3 us: local(): pre_grads = lax.all_gather(grads_part, 'row', axis=0, tiled=True)]
    pallas_call x0 -> x2, Pallas kernels: none -> 143 us  [the longest x1 130 us: main_call(): pl.pallas_call(main_kernel, out_shape=(jax.ShapeDtypeStruct((128, 512), B...]
    dot_general x5 -> x0, matrix products: 34.1 us -> none  [the longest x1 9.67 us: local(): jnp.dot(block, both_weights, preferred_element_type=jnp.float32)]
    all_to_all x1 -> x0, blocking collectives: 14.1 us -> none  [local(): lax.all_to_all(vision_tokens, 'row', split_axis=1, concat_axis=0, tiled=T...]
    gather x1 -> x0, local copies, waits for them, and re-layouts: 5.85 us -> none  [local(): inputs = jnp.take(pooled, pool_index, axis=0)]
  transfers between devices with their start and end apart: 7 -> 0, of which waited for: 7 -> 0; matrix products, arithmetic and copies ran while one was open for 6% -> 0% of each run, Pallas kernels for 0% -> 0%
where the time goes in v2:
time: 152 us; the launch traced here: 151 us
  Pallas kernels  143 us (94%)
  local copies, waits for them, and re-layouts  3.92 us (3%)
  other arithmetic  3.42 us (2%)
    pallas_call x1, Pallas kernels, main_call(): pl.pallas_call(main_kernel, out_shape=(jax.ShapeDtypeStruct((128, 512), B...  130 us
    pallas_call x1, Pallas kernels, grads_call(): pl.pallas_call(grads_kernel, grid=(1792 // width,), out_shape=(jax.ShapeD...  12.4 us

profile of v2, /device:TPU:1, one launch (start us, length us, event | category | flops | bytes accessed | tf_op | source)
XLA Modules:
  0.0 150.7 jit_solution(15631883226699669325)
XLA Ops:
  0.6 0.8 slice.7
  1.4 0.8 slice.6
  2.2 0.8 copy.20
  3.0 0.1 reduce-window.8
  3.1 0.1 reduce
  3.2 0.7 sub.33
  3.9 0.8 select_reduce_fusion.2
  4.7 0.2 copy.26
  5.0 0.2 copy.22
  5.2 0.2 copy.27
  5.4 0.2 copy.21
  5.7 1.7 %fusion.3.pos_ref = s32[1024,1]{1,0:T(8,128)} fusion(s32[1024,1]{1,0:T(8,128)S(1)} %copy.26, s32[1024,1]{1,0:T(8,128)S(1)} %copy.27, s32[1024,1]{1,0:T(8,128)S(1)} %copy.21, s32[1024,1]{1,0:T(8,128)S(1)} %copy.22), kind=kLoop, calls=%fused_computation.12 | loop fusion | flops 46080 | bytes 20480 | tf_op jit(solution)/shard_map/add | solution.py:580
  7.4 130.3 %row_sums.1 = (bf16[128,512]{1,0:T(8,128)(2,1)}, bf16[8,4,2,3,16,1792]{5,4,3,2,1,0:T(8,128)(2,1)}, bf16[8,128,512]{2,1,0:T(8,128)(2,1)}, bf16[8,128,512]{2,1,0:T(8,128)(2,1)}) custom-call(bf16[16,8192]{1,0:T(8,128)(2,1)} %v_ref.1, s32[1024,1]{1,0:T(8,128)} %fusion.3.pos_ref, bf16[128,512]{1,0:T(8,128)(2,1)} %og_ref.1, bf16[512,1792]{1,0:T(8,128)(2,1)} %gate_hbm.1, ...), custom_call_target="tpu_custom_call" | custom-call | flops 10000000000 | bytes 30000000 | tf_op jit(solution)/shard_map/row_sums/pallas_call | solution.py:503
  137.6 0.0 copy-start
  137.6 12.4 %weight_grads.1 = (f32[512,1792]{1,0:T(8,128)}, f32[512,1792]{1,0:T(8,128)}, f32[1792,512]{1,0:T(8,128)}) custom-call(bf16[8,128,512]{2,1,0:T(8,128)(2,1)} %get-tuple-element.12.x_ref, bf16[8,128,512]{2,1,0:T(8,128)(2,1)} %get-tuple-element.13.c_ref, bf16[8,4,2,3,16,1792]{5,4,3,2,1,0:T(8,128)(2,1)} %get-tuple-element.14.h_ref.gg_ref.ug_ref, ...), custom_call_target="tpu_custom_call" | custom-call | flops 6000000000 | bytes 24000000 | tf_op jit(solution)/shard_map/weight_grads/pallas_call | solution.py:547
  150.0 0.0 copy-done
  150.0 0.7 copy.29
  (1 shorter events, 0.0 us)
Async XLA Ops:
  137.6 12.4 %copy-start = (bf16[128,512]{1,0:T(8,128)(2,1)S(1)}, bf16[128,512]{1,0:T(8,128)(2,1)}, u32[]{:S(2)}) copy-start(bf16[128,512]{1,0:T(8,128)(2,1)} %get-tuple-element.26) | copy-start | bytes 393220

commit v3 on v2

--- a/solution.py
+++ b/solution.py
@@ -20,30 +20,11 @@
 AXY, AXP, AXM, AXF, AYP, AYM, AYF, AYY, CORE, XIN, CIN, LOZ = range(16, 28)
 KINDS = 28
 CP, CM, CY, CF1, CF2, DP, DM, DF1, DF2 = range(9)
-VY, VP, VM, WP, WM, VF1, VF2, VH, WF1, WF2 = range(9, 19)
-WG, WU, WD, LOY = range(19, 23)
-ONCE = 23
-FIRST = 7
-VR = 12
-
-def token_place(image_counts, image_owner, total):
-    position = jnp.arange(total, dtype=jnp.int32)
-    ends = jnp.cumsum(image_counts)
-    starts = ends - image_counts
-    member = ((position[:, None] >= starts[None, :]) & (position[:, None] < ends[None, :])).astype(
-        jnp.int32
-    )
-    count = jnp.sum(member * image_counts[None, :], axis=1)
-    begin = jnp.sum(member * starts[None, :], axis=1)
-    owner_first = jnp.sum(member * image_owner[0::2][None, :], axis=1)
-    owner_second = jnp.sum(member * image_owner[1::2][None, :], axis=1)
-    first = (count + 1) // 2
-    within = position - begin
-    second = (within >= first).astype(jnp.int32)
-    slot = within - second * first
-    owner = jnp.where(second > 0, owner_second, owner_first)
-    return (owner, slot)
-
+TP, TM, TY, TF1, TF2, UP, UM, UF1, UF2 = range(9, 18)
+RZ1, RZ2, RZ3, RZY, RY, RYZ1, RYZ2, RYZ3 = range(18, 26)
+WG, WU, WD, LOY = range(26, 30)
+ONCE = 30
+FIRST = 5
 
 def rem(a, n):
     return lax.rem(a, n)
@@ -57,9 +38,10 @@
 
 
 def main_kernel(
-    v_ref, pos_ref, og_ref, gate_hbm, up_hbm, down_hbm,
-    out_ref, o_ref, xo_ref, co_ref,
+    v_ref, counts_ref, owner_ref, og_ref, gate_hbm, up_hbm, down_hbm,
+    out_ref, o_ref, ht_ref, xt_ref, co_ref,
     act, pool, xin, c2, wg, wu, wd, wdo,
+    part, rtz, rty, stz, rtyz, rtzy, ht, xt,
     hfx, hfy, lo, rz, zs, rh,
     *rest,
 ):
@@ -101,7 +83,7 @@
     ]
     here[0].start()
     c2[col, :, 0:512] = og_ref[...]
-    pool[yh, z, row] = v_ref[:, pl.ds(pl.multiple_of(row * 512, 512), 512)]
+    pool[row] = v_ref[:, pl.ds(pl.multiple_of(row * 512, 512), 512)]
     pl.semaphore_wait(barrier, 19)
 
     cx = pl.ds(pl.multiple_of(k * HALF, 128), XW)
@@ -122,8 +104,11 @@
     def same(ref):
         return ref, ref
 
-    def cblk(hh, zz, lo_=0, n=128):
-        return c2.at[hh * 4 + zz, lo_:lo_ + n, 0:512]
+    def cblk(hh, zz, at=0, n=128):
+        return c2.at[hh * 4 + zz, at:at + n, 0:512]
+
+    def tblk(hh, zz, at=0, n=128):
+        return xin.at[hh * 4 + zz, at:at + n, 0:512]
 
     single = {
         WD: lambda: (down_hbm.at[theirs, :], wd.at[:, 512:1024], core_dev, wd.at[:, 512:1024]),
@@ -138,16 +123,23 @@
         DM: lambda: (*same(cblk(ho, z)), down_dev, cblk(ho, zp)),
         DF1: lambda: (*same(cblk(ho, zm, 0, 64)), up_dev, cblk(ho, zf, 0, 64)),
         DF2: lambda: (*same(cblk(ho, zp, 64, 64)), down_dev, cblk(ho, zf, 64, 64)),
-        VY: lambda: (*same(pool.at[yh, z, 0:VR]), hi_dev, pool.at[ho, z, 0:VR]),
-        VP: lambda: (*same(pool.at[yh, z, VR:16]), up_dev, pool.at[yh, zm, VR:16]),
-        VM: lambda: (*same(pool.at[yh, z, VR:16]), down_dev, pool.at[yh, zp, VR:16]),
-        VF1: lambda: (*same(pool.at[yh, zm, VR:VR + 2]), up_dev, pool.at[yh, zf, VR:VR + 2]),
-        VF2: lambda: (*same(pool.at[yh, zp, VR + 2:16]), down_dev, pool.at[yh, zf, VR + 2:16]),
-        VH: lambda: (*same(pool.at[yh, :, VR:16]), hi_dev, pool.at[ho, :, VR:16]),
-        WP: lambda: (*same(pool.at[:, z, 0:VR]), up_dev, pool.at[:, zm, 0:VR]),
-        WM: lambda: (*same(pool.at[:, z, 0:VR]), down_dev, pool.at[:, zp, 0:VR]),
-        WF1: lambda: (*same(pool.at[:, zm, 0:VR // 2]), up_dev, pool.at[:, zf, 0:VR // 2]),
-        WF2: lambda: (*same(pool.at[:, zp, VR // 2:VR]), down_dev, pool.at[:, zf, VR // 2:VR]),
+        TP: lambda: (*same(tblk(yh, z)), up_dev, tblk(yh, zm)),
+        TM: lambda: (*same(tblk(yh, z)), down_dev, tblk(yh, zp)),
+        TY: lambda: (*same(tblk(yh, z)), hi_dev, tblk(ho, z)),
+        TF1: lambda: (*same(tblk(yh, zm, 0, 64)), up_dev, tblk(yh, zf, 0, 64)),
+        TF2: lambda: (*same(tblk(yh, zp, 64, 64)), down_dev, tblk(yh, zf, 64, 64)),
+        UP: lambda: (*same(tblk(ho, z)), up_dev, tblk(ho, zm)),
+        UM: lambda: (*same(tblk(ho, z)), down_dev, tblk(ho, zp)),
+        UF1: lambda: (*same(tblk(ho, zm, 0, 64)), up_dev, tblk(ho, zf, 0, 64)),
+        UF2: lambda: (*same(tblk(ho, zp, 64, 64)), down_dev, tblk(ho, zf, 64, 64)),
+        RZ1: lambda: (part.at[:, zp, :, 0:256], rtz.at[0], at_col(yh, zp), rtz.at[0]),
+        RZ2: lambda: (part.at[:, zf, :, 0:256], rtz.at[1], at_col(yh, zf), rtz.at[1]),
+        RZ3: lambda: (part.at[:, zm, :, 0:256], rtz.at[2], at_col(yh, zm), rtz.at[2]),
+        RZY: lambda: (stz, rtzy, hi_dev, rtzy),
+        RY: lambda: (part.at[ho, :, :, 256:512], rty, hi_dev, rty),
+        RYZ1: lambda: (part.at[yh, zp, :, 256:512], rtyz.at[0], at_col(yh, zp), rtyz.at[0]),
+        RYZ2: lambda: (part.at[yh, zf, :, 256:512], rtyz.at[1], at_col(yh, zf), rtyz.at[1]),
+        RYZ3: lambda: (part.at[yh, zm, :, 256:512], rtyz.at[2], at_col(yh, zm), rtyz.at[2]),
         LOY: lambda: (zs, rh, hi_dev, rh),
     }
 
@@ -165,12 +157,17 @@
         s = 1 - 2 * rem(t, 2)
         return rem(x + s + 4, 4), rem(x - s + 4, 4)
 
+    def tokh(u):
+        there = jnp.where((u >= 2) & (u < 6), ho, yh)
+        off = jnp.where((u == 1) | (u == 3), 1, 0)
+        off = off + jnp.where((u == 4) | (u == 6), 3, 0) + jnp.where((u == 5) | (u == 7), 2, 0)
+        return there * 4 + rem(z + off, 4)
+
     def tok(t):
-        return rem(yh + 1 + t // 4, 2) * 4 + rem(z + 1 + rem(t, 4), 4)
-
-    def tokh(u):
-        w = rem(u, 4)
-        return rem(yh + u // 4, 2) * 4 + rem(z + w + (w // 2) * (5 - 2 * w), 4)
+        return tokh(rem(t + 1, 8))
+
+    def tokens(c):
+        return pl.ds(pl.multiple_of(c * 128, 128), 128)
 
     def table(kind, t):
         ahead, back = sides(t)
@@ -271,18 +268,88 @@
         hfx[c] = r3x(hg, u)[0]
         hfy[c] = r3y(hg, u)[0]
 
+    def place(c, ends, starts, counts, owners):
+        spot = lax.broadcasted_iota(jnp.int32, (128, 64), 0).astype(F32) + (c * 128).astype(F32)
+        member = jnp.where((spot >= starts) & (spot < ends), 1.0, 0.0)
+
+        def pick(values):
+            return jnp.sum(member * values, axis=1, keepdims=True).astype(jnp.int32)
+
+        count, begin = pick(counts), pick(starts)
+        within = lax.broadcasted_iota(jnp.int32, (128, 1), 0) + c * 128 - begin
+        first = (count + 1) >> 1
+        second = within >= first
+        slot = jnp.where(second, within - first, within)
+        owner = jnp.where(second, pick(owners[1]), pick(owners[0]))
+        index = jnp.where((owner & 7) == col, (owner >> 3) * 16 + slot, -1)
+        hot = jnp.where(lax.broadcasted_iota(jnp.int32, (128, 256), 1) == index, 1.0, 0.0).astype(BF)
+        rows = jnp.dot(hot, pool[...].reshape(256, 512), preferred_element_type=F32)
+        part[c // 4, rem(c, 4)] = rows.astype(BF)
+
+    def v_0():
+        lax.fori_loop(1, 16, spread_in, 0)
+        counts = jnp.broadcast_to(counts_ref[...].astype(F32), (8, 64))
+        owner = jnp.broadcast_to(owner_ref[...].astype(F32), (8, 128))
+        upto = lax.broadcasted_iota(jnp.int32, (64, 64), 0) <= lax.broadcasted_iota(jnp.int32, (64, 64), 1)
+        ends = jnp.dot(counts, jnp.where(upto, 1.0, 0.0), preferred_element_type=F32)
+        starts = ends - counts
+        i0 = lax.broadcasted_iota(jnp.int32, (128, 64), 0)
+        i1 = lax.broadcasted_iota(jnp.int32, (128, 64), 1) * 2
+        owners = [
+            jnp.dot(owner, jnp.where(i0 == i1 + j, 1.0, 0.0), preferred_element_type=F32)[0:1] for j in range(2)
+        ]
+
+        def body(c, carry):
+            place(c, ends[0:1], starts[0:1], counts[0:1], owners)
+            return carry
+
+        lax.fori_loop(0, 8, body, 0)
+        start1(RY, RZ1, RZ2, RZ3)
+
+    def v_2():
+        arrive1(RY)
+        part[yh, :, :, 256:512] = part[yh, :, :, 256:512] + rty[...]
+        start1(RYZ1, RYZ2, RYZ3)
+        arrive1(RZ1, RZ2, RZ3)
+        stz[...] = part[ho, z, :, 0:256] + rtz[0, ho] + rtz[1, ho] + rtz[2, ho]
+        start1(RZY)
+
+    def v_4():
+        arrive1(RYZ1, RYZ2, RYZ3)
+        xin[col, :, 256:512] = part[yh, z, :, 256:512] + rtyz[0] + rtyz[1] + rtyz[2]
+        arrive1(RZY)
+        xin[col, :, 0:256] = part[yh, z, :, 0:256] + rtz[0, yh] + rtz[1, yh] + rtz[2, yh] + rtzy[...]
+        start1(TP, TM, TY)
+
+    def t_0():
+        arrive1(TM)
+        start1(TF2)
+        arrive1(TY)
+        start1(UP, UM)
+        arrive1(TP)
+        start1(TF1)
+
+    def t_2():
+        arrive1(UP)
+        start1(UF1)
+        arrive1(UM)
+        start1(UF2)
+
+    def t_4():
+        arrive1(UF1, UF2)
+
+    def t_6():
+        arrive1(TF1, TF2)
+
     def p0(t):
-        c = tok(t)
-        spot = pos_ref[pl.ds(pl.multiple_of(c * 128, 128), 128), :]
-        pick = jnp.where(lax.broadcasted_iota(jnp.int32, (128, 2048), 1) == spot, 1.0, 0.0).astype(BF)
-        own = jnp.dot(pick, pool[...].reshape(2048, 512), preferred_element_type=F32)
-        xin[c, :, 0:512] = own.astype(BF)
         start(t, XIN)
-        pltpu.make_async_copy(xin.at[c, :, 0:512], xo_ref.at[c], osem.at[1, t]).start()
 
     def s0(t):
         arrive(t, XIN)
-        x_t = xin[tok(t)]
+        c = tok(t)
+        x_t = xin[c]
+        xt[t] = x_t[:, 0:512].T
+        pltpu.make_async_copy(xt.at[t], xt_ref.at[:, tokens(c)], osem.at[1, t]).start()
         r0(gu, t, [jnp.dot(x_t, w[...], preferred_element_type=F32) for w in (wg, wu)])
 
     def activate(c, full, hgrad, cols):
@@ -320,42 +387,45 @@
     def s7(t):
         c = tok(t)
         arrive(t, CORE)
-        pltpu.make_async_copy(act.at[c], o_ref.at[c], osem.at[0, t]).start()
+        pltpu.make_async_copy(act.at[c, :, :, 1:3], o_ref.at[c], osem.at[0, t]).start()
         hidden = act[c, :, :, 0].reshape(128, 2 * HALF)
         lo[t] = jnp.dot(hidden, wdo[...], preferred_element_type=F32)
 
-        @pl.when(rem(t, 4) < 3)
+        @pl.when((t != 1) & (t != 7))
         def _():
             start(t, LOZ)
 
+        ht[t] = hidden.T
+        pltpu.make_async_copy(ht.at[t], ht_ref.at[:, tokens(c)], osem.at[2, t]).start()
+
         @pl.when(t == 7)
         def _():
-            arrive(4, LOZ)
+            arrive(0, LOZ)
             arrive(5, LOZ)
             arrive(6, LOZ)
             arrive1(LOY)
-            out_ref[...] = (lo[7] + rz[4] + rz[5] + rz[6] + rh[...]).astype(BF)
+            out_ref[...] = (lo[7] + rz[0] + rz[5] + rz[6] + rh[...]).astype(BF)
 
     def s8(t):
-        @pl.when(t == 3)
+        @pl.when(t == 4)
         def _():
-            arrive(0, LOZ)
-            arrive(1, LOZ)
             arrive(2, LOZ)
-            zs[...] = lo[3] + rz[0] + rz[1] + rz[2]
+            arrive(3, LOZ)
+            arrive(4, LOZ)
+            zs[...] = lo[1] + rz[2] + rz[3] + rz[4]
             start1(LOY)
 
     def spread(i, carry):
         to = rem(row + i, 16)
         pltpu.make_async_remote_copy(
             src_ref=v_ref.at[:, pl.ds(pl.multiple_of(to * 512, 512), 512)],
-            dst_ref=pool.at[yh, z, row],
+            dst_ref=pool.at[row],
             send_sem=sa.at[i], recv_sem=ra.at[i], device_id={"row": to}, device_id_type=MESH,
         ).start()
         return carry
 
     def spread_in(i, carry):
-        place = pool.at[yh, z, rem(row + 16 - i, 16)]
+        place = pool.at[rem(row + 16 - i, 16)]
         pltpu.make_async_remote_copy(
             src_ref=place, dst_ref=place, send_sem=sa.at[i], recv_sem=ra.at[i],
             device_id=y_dev, device_id_type=MESH,
@@ -365,7 +435,7 @@
     def spread_out(i, carry):
         place = v_ref.at[:, 0:512]
         pltpu.make_async_remote_copy(
-            src_ref=place, dst_ref=pool.at[yh, z, row], send_sem=sa.at[i], recv_sem=ra.at[i],
+            src_ref=place, dst_ref=pool.at[row], send_sem=sa.at[i], recv_sem=ra.at[i],
             device_id=y_dev, device_id_type=MESH,
         ).wait_send()
         return carry
@@ -376,45 +446,25 @@
         c.start()
 
     def c_1():
-        arrive1(CP)
-        start1(CF1)
         arrive1(CM)
         start1(CF2)
         arrive1(CY)
         start1(DP, DM)
+        arrive1(CP)
+        start1(CF1)
 
     def c_3():
-        arrive1(CF1, CF2, DP)
+        arrive1(DP)
         start1(DF1)
         arrive1(DM)
         start1(DF2)
 
+    def c_5():
+        arrive1(DF1, DF2)
+
     def c_7():
-        arrive1(DF1, DF2)
+        arrive1(CF1, CF2)
         pltpu.make_async_copy(c2.at[:, :, 0:512], co_ref, lsem.at[4]).start()
-
-    def v_0():
-        lax.fori_loop(1, 16, spread_in, 0)
-        start1(VY, VP, VM)
-
-    def v_2():
-        arrive1(VY)
-        start1(WP, WM)
-        arrive1(VP)
-        start1(VF1)
-        arrive1(VM)
-        start1(VF2)
-
-    def v_4():
-        arrive1(VF1, VF2)
-        start1(VH)
-        arrive1(WP)
-        start1(WF1)
-        arrive1(WM)
-        start1(WF2)
-
-    def v_6():
-        arrive1(WF1, WF2, VH)
 
     def w_1():
         here[0].wait()
@@ -442,6 +492,7 @@
     def step(n, carry):
         at(n, 1, c_1)
         at(n, 3, c_3)
+        at(n, 5, c_5)
         at(n, 7, c_7)
         at(n, 1, w_1)
         for lag, stage in enumerate(
@@ -451,7 +502,10 @@
         at(n, 0, v_0)
         at(n, 2, v_2)
         at(n, 4, v_4)
-        at(n, 6, v_6)
+        at(n, FIRST, t_0)
+        at(n, FIRST + 2, t_2)
+        at(n, FIRST + 4, t_4)
+        at(n, FIRST + 6, t_6)
         at(n, FIRST + 1, w_8)
         for lag, stage in enumerate(
             [p0, s0, lambda t: r1(gu, t), lambda t: r2(gu, t), s3, s4, s5, s6, s7, s8]
@@ -470,13 +524,14 @@
             if kind != LOZ:
                 sent(kind, t)
 
-        @pl.when(rem(t, 4) < 3)
+        @pl.when((t != 1) & (t != 7))
         def _():
             sent(LOZ, t)
 
         c = tok(t)
-        pltpu.make_async_copy(act.at[c], o_ref.at[c], osem.at[0, t]).wait()
-        pltpu.make_async_copy(xin.at[c, :, 0:512], xo_ref.at[c], osem.at[1, t]).wait()
+        pltpu.make_async_copy(act.at[c, :, :, 1:3], o_ref.at[c], osem.at[0, t]).wait()
+        pltpu.make_async_copy(ht.at[t], ht_ref.at[:, tokens(c)], osem.at[2, t]).wait()
+        pltpu.make_async_copy(xt.at[t], xt_ref.at[:, tokens(c)], osem.at[1, t]).wait()
         return carry
 
     lax.fori_loop(0, CHUNKS, finish, 0)
@@ -487,7 +542,7 @@
     pltpu.make_async_copy(c2.at[:, :, 0:512], co_ref, lsem.at[4]).wait()
 
 
-def main_call(v, pos, og, gate, up, down):
+def main_call(v, counts, owner, og, gate, up, down):
     n = CHUNKS
     vm = lambda *s: pltpu.VMEM(s, BF)
     vf = lambda *s: pltpu.VMEM(s, F32)
@@ -504,43 +559,40 @@
         main_kernel,
         out_shape=(
             jax.ShapeDtypeStruct((128, 512), BF),
-            jax.ShapeDtypeStruct((n, 4, 2, 3, 16, 2 * HALF), BF),
-            jax.ShapeDtypeStruct((n, 128, 512), BF),
+            jax.ShapeDtypeStruct((n, 4, 2, 2, 16, 2 * HALF), BF),
+            jax.ShapeDtypeStruct((2 * HALF, 1024), BF),
+            jax.ShapeDtypeStruct((512, 1024), BF),
             jax.ShapeDtypeStruct((n, 128, 512), BF),
         ),
-        in_specs=[vmem, vmem, vmem, hbm, hbm, hbm],
-        out_specs=(vmem, hbm, hbm, hbm),
+        in_specs=[vmem, vmem, vmem, vmem, hbm, hbm, hbm],
+        out_specs=(vmem, hbm, hbm, hbm, hbm),
         scratch_shapes=[
-            vm(n, 4, 2, 3, 16, 2 * HALF), vm(2, 4, 16, 16, 512), vm(n, 128, 1024), vm(n, 128, 1024),
+            vm(n, 4, 2, 3, 16, 2 * HALF), vm(16, 16, 512), vm(n, 128, 1024), vm(n, 128, 1024),
             vm(1024, HALF), vm(1024, HALF), vm(HALF, 1024), vm(2 * HALF, 512),
+            vm(2, 4, 128, 512), vm(3, 2, 128, 256), vm(4, 128, 256), vm(128, 256), vm(3, 128, 256), vm(128, 256),
+            vm(n, 2 * HALF, 128), vm(n, 512, 128),
             vf(n, 16, XW), vf(n, 16, YW),
             vf(n, 128, 512), vf(n, 128, 512), vf(128, 512), vf(128, 512),
             *row_sum(2), *row_sum(1),
             dma((KINDS, n)), dma((KINDS, n)), dma((ONCE,)), dma((ONCE,)), dma((16,)), dma((16,)),
-            dma((2, n)), dma((5,)),
+            dma((3, n)), dma((5,)),
         ],
         compiler_params=pltpu.CompilerParams(
             collective_id=0, has_side_effects=True, vmem_limit_bytes=60 << 20
         ),
         cost_estimate=pl.CostEstimate(flops=10**10, bytes_accessed=30 * 10**6, transcendentals=0),
         name="row_sums",
-    )(v, pos, og, gate, up, down)
-
-
-def grads_kernel(x_ref, c_ref, h_ref, gg_ref, ug_ref, gate_ref, up_ref, down_ref, xt):
-    @pl.when(pl.program_id(0) == 0)
-    def _():
-        xt[...] = x_ref[...].reshape(1024, 512).T
-
-    width = h_ref.shape[-1]
-    gate_ref[...] = jnp.dot(xt[...], gg_ref[...].reshape(1024, width), preferred_element_type=F32)
-    up_ref[...] = jnp.dot(xt[...], ug_ref[...].reshape(1024, width), preferred_element_type=F32)
-    down_ref[...] = lax.dot_general(
-        h_ref[...].reshape(1024, width), c_ref[...].reshape(1024, 512), (((0,), (0,)), ((), ())), preferred_element_type=F32
-    )
-
-
-def grads_call(x, c, o):
+    )(v, counts, owner, og, gate, up, down)
+
+
+def grads_kernel(xt_ref, c_ref, ht_ref, gg_ref, ug_ref, gate_ref, up_ref, down_ref):
+    width = ht_ref.shape[0]
+    gate_ref[...] = jnp.dot(xt_ref[...], gg_ref[...].reshape(1024, width), preferred_element_type=F32)
+    up_ref[...] = jnp.dot(xt_ref[...], ug_ref[...].reshape(1024, width), preferred_element_type=F32)
+    down_ref[...] = jnp.dot(ht_ref[...], c_ref[...].reshape(1024, 512), preferred_element_type=F32)
+
+
+def grads_call(xt, c, ht, o):
     width = 256
     n = CHUNKS
     part = lambda m: pl.BlockSpec((n, 4, 2, 1, 16, width), lambda j: (0, 0, 0, m, 0, j))
@@ -553,35 +605,27 @@
             jax.ShapeDtypeStruct((1792, 512), F32),
         ),
         in_specs=[
+            pl.BlockSpec((512, 1024), lambda j: (0, 0)),
             pl.BlockSpec((n, 128, 512), lambda j: (0, 0, 0)),
-            pl.BlockSpec((n, 128, 512), lambda j: (0, 0, 0)),
-            part(0), part(1), part(2),
+            pl.BlockSpec((width, 1024), lambda j: (j, 0)),
+            part(0), part(1),
         ],
         out_specs=(
             pl.BlockSpec((512, width), lambda j: (0, j)),
             pl.BlockSpec((512, width), lambda j: (0, j)),
             pl.BlockSpec((width, 512), lambda j: (j, 0)),
         ),
-        scratch_shapes=[pltpu.VMEM((512, 1024), BF)],
         compiler_params=pltpu.CompilerParams(vmem_limit_bytes=60 << 20),
         cost_estimate=pl.CostEstimate(flops=6 * 10**9, bytes_accessed=24 * 10**6, transcendentals=0),
         name="weight_grads",
-    )(x, c, o, o, o)
+    )(xt, c, ht, o, o)
 
 
 def local(vision_tokens, image_counts, image_owner, gate_weight, up_weight, down_weight, out_grad):
-    slots = vision_tokens.shape[0]
-    row_count = lax.axis_size("row")
-    col_count = lax.axis_size("col")
-    token_total = out_grad.shape[0] * col_count
-    owner, slot = token_place(image_counts, image_owner, token_total)
-    owner_row = owner // col_count
-    owner_col = owner % col_count
-    pool_index = owner_col * (row_count * slots) + owner_row * slots + slot
-    layer_out, o, x, c = main_call(
-        vision_tokens, pool_index[:, None], out_grad, gate_weight, up_weight, down_weight
+    layer_out, o, ht, xt, c = main_call(
+        vision_tokens, image_counts[None, :], image_owner[None, :], out_grad, gate_weight, up_weight, down_weight
     )
-    grad_gate, grad_up, grad_down = grads_call(x, c, o)
+    grad_gate, grad_up, grad_down = grads_call(xt, c, ht, o)
     return (layer_out, grad_gate, grad_up, grad_down)
 
 

time: 152 us -> 141 us (0.928)
  Pallas kernels: 143 us -> 137 us
  other arithmetic: 3.42 us -> 0 us
  local copies, waits for them, and re-layouts: 3.92 us -> 0.66 us
    pallas_call x1, Pallas kernels: 130 us -> 125 us  [main_call(): pl.pallas_call(main_kernel, out_shape=(jax.ShapeDtypeStruct((128, 512), B...]
    add x2 -> x0, other arithmetic: 1.7 us -> none  [the longest x1 1.7 us: local(): pool_index = owner_col * (row_count * slots) + owner_row * slots + slot]
    slice x2 -> x0, local copies, waits for them, and re-layouts: 1.61 us -> none  [the longest x1 0.81 us: token_place(): owner_second = jnp.sum(member * image_owner[1::2][None, :], axis=1)]
where the time goes in v3:
time: 141 us; the launch traced here: 139 us
  Pallas kernels  137 us (97%)
    pallas_call x1, Pallas kernels, main_call(): pl.pallas_call(main_kernel, out_shape=(jax.ShapeDtypeStruct((128, 512), B...  125 us
    pallas_call x1, Pallas kernels, grads_call(): pl.pallas_call(grads_kernel, grid=(1792 // width,), out_shape=(jax.ShapeD...  12 us

profile of v3, /device:TPU:1, one launch (start us, length us, event | category | flops | bytes accessed | tf_op | source)
XLA Modules:
  0.0 138.6 jit_solution(14217608564318917082)
XLA Ops:
  0.6 125.3 %row_sums.1 = (bf16[128,512]{1,0:T(8,128)(2,1)}, bf16[8,4,2,2,16,1792]{5,4,3,2,1,0:T(8,128)(2,1)}, bf16[1792,1024]{1,0:T(8,128)(2,1)}, bf16[512,1024]{1,0:T(8,128)(2,1)}, bf16[8,128,512]{2,1,0:T(8,128)(2,1)}) custom-call(bf16[16,8192]{1,0:T(8,128)(2,1)} %v_ref.1, s32[1,64]{1,0:T(1,128)} %bitcast.2, s32[1,128]{1,0:T(1,128)} %bitcast.3, ...), custom_call_target="tpu_custom_call" | custom-call | flops 10000000000 | bytes 30000000 | tf_op jit(solution)/shard_map/row_sums/pallas_call | solution.py:558
  125.9 0.0 copy-start
  125.9 12.0 %weight_grads.1 = (f32[512,1792]{1,0:T(8,128)}, f32[512,1792]{1,0:T(8,128)}, f32[1792,512]{1,0:T(8,128)}) custom-call(bf16[512,1024]{1,0:T(8,128)(2,1)} %get-tuple-element.13.xt_ref, bf16[8,128,512]{2,1,0:T(8,128)(2,1)} %get-tuple-element.14.c_ref, bf16[1792,1024]{1,0:T(8,128)(2,1)} %get-tuple-element.15.ht_ref, ...), custom_call_target="tpu_custom_call" | custom-call | flops 6000000000 | bytes 24000000 | tf_op jit(solution)/shard_map/weight_grads/pallas_call | solution.py:599
  137.9 0.0 copy-done
  138.0 0.7 copy.12
Async XLA Ops:
  125.9 12.0 %copy-start = (bf16[128,512]{1,0:T(8,128)(2,1)S(1)}, bf16[128,512]{1,0:T(8,128)(2,1)}, u32[]{:S(2)}) copy-start(bf16[128,512]{1,0:T(8,128)(2,1)} %get-tuple-element.24) | copy-start | bytes 393220

commit v4 on v3

--- a/solution.py
+++ b/solution.py
@@ -22,8 +22,9 @@
 CP, CM, CY, CF1, CF2, DP, DM, DF1, DF2 = range(9)
 TP, TM, TY, TF1, TF2, UP, UM, UF1, UF2 = range(9, 18)
 RZ1, RZ2, RZ3, RZY, RY, RYZ1, RYZ2, RYZ3 = range(18, 26)
-WG, WU, WD, LOY = range(26, 30)
-ONCE = 30
+WG, WU, WD, LOY, AXL, AYL = range(26, 32)
+ONCE = 32
+SLOTS = 4
 FIRST = 5
 
 def rem(a, n):
@@ -41,12 +42,12 @@
     v_ref, counts_ref, owner_ref, og_ref, gate_hbm, up_hbm, down_hbm,
     out_ref, o_ref, ht_ref, xt_ref, co_ref,
     act, pool, xin, c2, wg, wu, wd, wdo,
-    part, rtz, rty, stz, rtyz, rtzy, ht, xt,
+    hot, part, rtz, rty, stz, rtyz, rtzy, ht, xt,
     hfx, hfy, lo, rz, zs, rh,
     *rest,
 ):
     gu, hg = RowSum(0, rest[:18]), RowSum(HG, rest[18:36])
-    ssem, rsem, ssem1, rsem1, sa, ra, osem, lsem = rest[36:]
+    ssem, rsem, zsem, ssem1, rsem1, asem, osem, lsem = rest[36:]
     row = lax.axis_index("row")
     col = lax.axis_index("col")
     x, y, k = row // 4, rem(row // 2, 2), rem(row, 2)
@@ -62,6 +63,7 @@
         return {"col": hh * 4 + zz}
 
     y_dev, core_dev = at_row(x, yo, k), at_row(x, y, ko)
+    far_dev = at_row(far, y, k)
     up_dev, down_dev, hi_dev = at_col(yh, zp), at_col(yh, zm), at_col(ho, z)
     barrier = pltpu.get_barrier_semaphore()
 
@@ -91,7 +93,7 @@
 
     def copy(kind, t, src, dst, dev):
         return pltpu.make_async_remote_copy(
-            src_ref=src, dst_ref=dst, send_sem=ssem.at[kind, t], recv_sem=rsem.at[kind, t],
+            src_ref=src, dst_ref=dst, send_sem=ssem.at[kind], recv_sem=rsem.at[kind, rem(t, SLOTS)] if kind != LOZ else zsem.at[t],
             device_id=dev, device_id_type=MESH,
         )
 
@@ -141,6 +143,8 @@
         RYZ2: lambda: (part.at[yh, zf, :, 256:512], rtyz.at[1], at_col(yh, zf), rtyz.at[1]),
         RYZ3: lambda: (part.at[yh, zm, :, 256:512], rtyz.at[2], at_col(yh, zm), rtyz.at[2]),
         LOY: lambda: (zs, rh, hi_dev, rh),
+        AXL: lambda: (*same(act.at[col, x, :, :, :, cx]), far_dev, act.at[col, far, :, :, :, cx]),
+        AYL: lambda: (*same(act.at[col, x, y, :, :, cy]), far_dev, act.at[col, far, y, :, :, cy]),
     }
 
     def start1(*kinds):
@@ -256,9 +260,6 @@
         arrive(t, r.base + YD, r.base + Y2)
         return r.py[b, y, x] + r.ryd[t].astype(F32) + r.ry2[t].astype(F32)
 
-    def hx(u):
-        start(u, CIN)
-
     def h0(u):
         arrive(u, CIN)
         r0(hg, u, [lax.dot_general(c2[tokh(u)], wd[...], (((1,), (1,)), ((), ())), preferred_element_type=F32)])
@@ -282,12 +283,9 @@
         slot = jnp.where(second, within - first, within)
         owner = jnp.where(second, pick(owners[1]), pick(owners[0]))
         index = jnp.where((owner & 7) == col, (owner >> 3) * 16 + slot, -1)
-        hot = jnp.where(lax.broadcasted_iota(jnp.int32, (128, 256), 1) == index, 1.0, 0.0).astype(BF)
-        rows = jnp.dot(hot, pool[...].reshape(256, 512), preferred_element_type=F32)
-        part[c // 4, rem(c, 4)] = rows.astype(BF)
-
-    def v_0():
-        lax.fori_loop(1, 16, spread_in, 0)
+        hot[c] = jnp.where(lax.broadcasted_iota(jnp.int32, (128, 256), 1) == index, 1.0, 0.0).astype(BF)
+
+    def find_places():
         counts = jnp.broadcast_to(counts_ref[...].astype(F32), (8, 64))
         owner = jnp.broadcast_to(owner_ref[...].astype(F32), (8, 128))
         upto = lax.broadcasted_iota(jnp.int32, (64, 64), 0) <= lax.broadcasted_iota(jnp.int32, (64, 64), 1)
@@ -304,6 +302,11 @@
             return carry
 
         lax.fori_loop(0, 8, body, 0)
+
+    def v_0():
+        spread_all().wait_recv()
+        rows = jnp.dot(hot[...].reshape(1024, 256), pool[...].reshape(256, 512), preferred_element_type=F32)
+        part[...] = rows.astype(BF).reshape(2, 4, 128, 512)
         start1(RY, RZ1, RZ2, RZ3)
 
     def v_2():
@@ -314,7 +317,7 @@
         stz[...] = part[ho, z, :, 0:256] + rtz[0, ho] + rtz[1, ho] + rtz[2, ho]
         start1(RZY)
 
-    def v_4():
+    def v_3():
         arrive1(RYZ1, RYZ2, RYZ3)
         xin[col, :, 256:512] = part[yh, z, :, 256:512] + rtyz[0] + rtyz[1] + rtyz[2]
         arrive1(RZY)
@@ -349,7 +352,7 @@
         c = tok(t)
         x_t = xin[c]
         xt[t] = x_t[:, 0:512].T
-        pltpu.make_async_copy(xt.at[t], xt_ref.at[:, tokens(c)], osem.at[1, t]).start()
+        pltpu.make_async_copy(xt.at[t], xt_ref.at[:, tokens(c)], osem.at[1]).start()
         r0(gu, t, [jnp.dot(x_t, w[...], preferred_element_type=F32) for w in (wg, wu)])
 
     def activate(c, full, hgrad, cols):
@@ -366,28 +369,70 @@
         activate(c, r3y(gu, t), hfy[c], cy)
         start(t, AYP, AYM)
 
+        @pl.when(t == 7)
+        def _():
+            start1(AYL)
+
     def s4(t):
         arrive(t, AXY)
         start(t, AXP, AXM)
+
+        @pl.when(t == 7)
+        def _():
+            start1(AXL)
+
         arrive(t, AYP)
-        start(t, AYF)
+
+        @pl.when(t < 7)
+        def _():
+            start(t, AYF)
+
         arrive(t, AYM)
+
+        @pl.when(t == 7)
+        def _():
+            arrive1(AYL)
+            start(t, AYY)
 
     def s5(t):
         arrive(t, AXP)
-        start(t, AXF)
+
+        @pl.when(t < 7)
+        def _():
+            start(t, AXF)
+
         arrive(t, AXM)
-        arrive(t, AYF)
-        start(t, AYY)
+
+        @pl.when(t < 7)
+        def _():
+            arrive(t, AYF)
+            start(t, AYY)
+
+        @pl.when(t == 7)
+        def _():
+            arrive1(AXL)
+            arrive(t, AYY)
+            start(t, CORE)
 
     def s6(t):
-        arrive(t, AXF, AYY)
-        start(t, CORE)
+        @pl.when(t < 7)
+        def _():
+            arrive(t, AXF, AYY)
+            start(t, CORE)
+
+        @pl.when(t == 7)
+        def _():
+            project(t)
 
     def s7(t):
+        @pl.when(t < 7)
+        def _():
+            project(t)
+
+    def project(t):
         c = tok(t)
         arrive(t, CORE)
-        pltpu.make_async_copy(act.at[c, :, :, 1:3], o_ref.at[c], osem.at[0, t]).start()
+        pltpu.make_async_copy(act.at[c, :, :, 1:3], o_ref.at[c], osem.at[0]).start()
         hidden = act[c, :, :, 0].reshape(128, 2 * HALF)
         lo[t] = jnp.dot(hidden, wdo[...], preferred_element_type=F32)
 
@@ -396,15 +441,7 @@
             start(t, LOZ)
 
         ht[t] = hidden.T
-        pltpu.make_async_copy(ht.at[t], ht_ref.at[:, tokens(c)], osem.at[2, t]).start()
-
-        @pl.when(t == 7)
-        def _():
-            arrive(0, LOZ)
-            arrive(5, LOZ)
-            arrive(6, LOZ)
-            arrive1(LOY)
-            out_ref[...] = (lo[7] + rz[0] + rz[5] + rz[6] + rh[...]).astype(BF)
+        pltpu.make_async_copy(ht.at[t], ht_ref.at[:, tokens(c)], osem.at[2]).start()
 
     def s8(t):
         @pl.when(t == 4)
@@ -420,32 +457,17 @@
         pltpu.make_async_remote_copy(
             src_ref=v_ref.at[:, pl.ds(pl.multiple_of(to * 512, 512), 512)],
             dst_ref=pool.at[row],
-            send_sem=sa.at[i], recv_sem=ra.at[i], device_id={"row": to}, device_id_type=MESH,
+            send_sem=asem.at[0], recv_sem=asem.at[1], device_id={"row": to}, device_id_type=MESH,
         ).start()
         return carry
 
-    def spread_in(i, carry):
-        place = pool.at[rem(row + 16 - i, 16)]
-        pltpu.make_async_remote_copy(
-            src_ref=place, dst_ref=place, send_sem=sa.at[i], recv_sem=ra.at[i],
+    def spread_all():
+        return pltpu.make_async_remote_copy(
+            src_ref=pool.at[0:15], dst_ref=pool.at[0:15], send_sem=asem.at[0], recv_sem=asem.at[1],
             device_id=y_dev, device_id_type=MESH,
-        ).wait_recv()
-        return carry
-
-    def spread_out(i, carry):
-        place = v_ref.at[:, 0:512]
-        pltpu.make_async_remote_copy(
-            src_ref=place, dst_ref=pool.at[row], send_sem=sa.at[i], recv_sem=ra.at[i],
-            device_id=y_dev, device_id_type=MESH,
-        ).wait_send()
-        return carry
-
-    lax.fori_loop(1, 16, spread, 0)
-    start1(WD, CP, CM, CY)
-    for c in here[1:]:
-        c.start()
-
-    def c_1():
+        )
+
+    def c_0():
         arrive1(CM)
         start1(CF2)
         arrive1(CY)
@@ -453,30 +475,37 @@
         arrive1(CP)
         start1(CF1)
 
-    def c_3():
+    def c_2():
         arrive1(DP)
         start1(DF1)
         arrive1(DM)
         start1(DF2)
 
-    def c_5():
+    def c_4():
         arrive1(DF1, DF2)
 
-    def c_7():
+    def c_6():
         arrive1(CF1, CF2)
         pltpu.make_async_copy(c2.at[:, :, 0:512], co_ref, lsem.at[4]).start()
 
-    def w_1():
+    def w_0():
         here[0].wait()
         arrive1(WD)
         start1(WG, WU)
 
-    def w_8():
+    def w_1():
         here[1].wait()
         here[2].wait()
         here[3].wait()
         arrive1(WG, WU)
 
+    start(0, CIN)
+    lax.fori_loop(1, 16, spread, 0)
+    start1(WD, CP, CM, CY)
+    find_places()
+    for c in here[1:]:
+        c.start()
+
     def each(n, lag, stage):
         t = n - lag
 
@@ -490,55 +519,64 @@
             stage()
 
     def step(n, carry):
-        at(n, 1, c_1)
-        at(n, 3, c_3)
-        at(n, 5, c_5)
-        at(n, 7, c_7)
-        at(n, 1, w_1)
-        for lag, stage in enumerate(
-            [hx, h0, lambda u: r1(hg, u), lambda u: r2(hg, u), h3]
-        ):
+        at(n, 0, w_0)
+        for lag, stage in enumerate([h0, lambda u: r1(hg, u), lambda u: r2(hg, u), h3]):
             each(n, lag, stage)
+        at(n, 0, c_0)
+        at(n, 2, c_2)
+        at(n, 4, c_4)
+        at(n, 6, c_6)
+
+        @pl.when(n < CHUNKS - 1)
+        def _():
+            start(n + 1, CIN)
+
         at(n, 0, v_0)
         at(n, 2, v_2)
-        at(n, 4, v_4)
+        at(n, 3, v_3)
         at(n, FIRST, t_0)
         at(n, FIRST + 2, t_2)
         at(n, FIRST + 4, t_4)
         at(n, FIRST + 6, t_6)
-        at(n, FIRST + 1, w_8)
-        for lag, stage in enumerate(
-            [p0, s0, lambda t: r1(gu, t), lambda t: r2(gu, t), s3, s4, s5, s6, s7, s8]
-        ):
+        at(n, FIRST + 1, w_1)
+        for lag, stage in [
+            (0, p0), (1, s0), (2, lambda t: r1(gu, t)), (3, lambda t: r2(gu, t)), (4, s3), (5, s4), (6, s5),
+            (8, s7), (7, s6), (9, s8),
+        ]:
             each(n, FIRST + lag, stage)
         return carry
 
-    lax.fori_loop(0, FIRST + CHUNKS + 9, step, 0)
-
-    def sent(kind, t):
-        src, dst, dev, _ = table(kind, t)
-        copy(kind, t, src, dst, dev).wait_send()
-
-    def finish(t, carry):
-        for kind in range(KINDS):
-            if kind != LOZ:
-                sent(kind, t)
-
-        @pl.when((t != 1) & (t != 7))
-        def _():
-            sent(LOZ, t)
-
-        c = tok(t)
-        pltpu.make_async_copy(act.at[c, :, :, 1:3], o_ref.at[c], osem.at[0, t]).wait()
-        pltpu.make_async_copy(ht.at[t], ht_ref.at[:, tokens(c)], osem.at[2, t]).wait()
-        pltpu.make_async_copy(xt.at[t], xt_ref.at[:, tokens(c)], osem.at[1, t]).wait()
-        return carry
-
-    lax.fori_loop(0, CHUNKS, finish, 0)
-    lax.fori_loop(1, 16, spread_out, 0)
+    lax.fori_loop(0, FIRST + CHUNKS + 7, step, 0)
+    arrive(0, LOZ)
+    arrive(5, LOZ)
+    arrive(6, LOZ)
+    arrive1(LOY)
+    out_ref[...] = (lo[7] + rz[0] + rz[5] + rz[6] + rh[...]).astype(BF)
+
+    def all_sent(kind):
+        if kind < 16:
+            r = gu if kind < HG else hg
+            return (r.sxd, r.sxr, r.sx2, r.sxy, r.syy, r.syd, r.syr, r.sy2)[kind % HG]
+        if kind in (AXP, AXM, AXF):
+            return act.at[0:7 if kind == AXF else 8, x, :, :, :, cx]
+        if kind in (AYP, AYM, AYF):
+            return act.at[0:7 if kind == AYF else 8, x, y, :, :, cy]
+        return {
+            AXY: lambda: act.at[:, x, y, :, :, cx], AYY: lambda: act.at[:, :, y, :, :, cy],
+            CORE: lambda: act.at[:, :, :, :, :, mine], XIN: lambda: xin.at[:, :, 0:512],
+            CIN: lambda: c2.at[:, :, 0:512], LOZ: lambda: lo.at[0:6],
+        }[kind]()
+
+    for kind in range(KINDS):
+        ref = all_sent(kind)
+        copy(kind, 0, ref, ref, y_dev).wait_send()
     for kind in range(ONCE):
         src, dst, dev, _ = single[kind]()
         once(kind, src, dst, dev).wait_send()
+    spread_all().wait_send()
+    pltpu.make_async_copy(act.at[:, :, :, 1:3], o_ref, osem.at[0]).wait()
+    pltpu.make_async_copy(xt, xt, osem.at[1]).wait()
+    pltpu.make_async_copy(ht, ht, osem.at[2]).wait()
     pltpu.make_async_copy(c2.at[:, :, 0:512], co_ref, lsem.at[4]).wait()
 
 
@@ -569,13 +607,13 @@
         scratch_shapes=[
             vm(n, 4, 2, 3, 16, 2 * HALF), vm(16, 16, 512), vm(n, 128, 1024), vm(n, 128, 1024),
             vm(1024, HALF), vm(1024, HALF), vm(HALF, 1024), vm(2 * HALF, 512),
-            vm(2, 4, 128, 512), vm(3, 2, 128, 256), vm(4, 128, 256), vm(128, 256), vm(3, 128, 256), vm(128, 256),
+            vm(8, 128, 256), vm(2, 4, 128, 512), vm(3, 2, 128, 256), vm(4, 128, 256), vm(128, 256), vm(3, 128, 256), vm(128, 256),
             vm(n, 2 * HALF, 128), vm(n, 512, 128),
             vf(n, 16, XW), vf(n, 16, YW),
             vf(n, 128, 512), vf(n, 128, 512), vf(128, 512), vf(128, 512),
             *row_sum(2), *row_sum(1),
-            dma((KINDS, n)), dma((KINDS, n)), dma((ONCE,)), dma((ONCE,)), dma((16,)), dma((16,)),
-            dma((3, n)), dma((5,)),
+            dma((KINDS,)), dma((KINDS, SLOTS)), dma((n,)), dma((ONCE,)), dma((ONCE,)), dma((2,)),
+            dma((3,)), dma((5,)),
         ],
         compiler_params=pltpu.CompilerParams(
             collective_id=0, has_side_effects=True, vmem_limit_bytes=60 << 20
@@ -585,40 +623,66 @@
     )(v, counts, owner, og, gate, up, down)
 
 
-def grads_kernel(xt_ref, c_ref, ht_ref, gg_ref, ug_ref, gate_ref, up_ref, down_ref):
-    width = ht_ref.shape[0]
-    gate_ref[...] = jnp.dot(xt_ref[...], gg_ref[...].reshape(1024, width), preferred_element_type=F32)
-    up_ref[...] = jnp.dot(xt_ref[...], ug_ref[...].reshape(1024, width), preferred_element_type=F32)
-    down_ref[...] = jnp.dot(ht_ref[...], c_ref[...].reshape(1024, 512), preferred_element_type=F32)
+def grads_kernel(xt_ref, c_ref, ht_ref, o_ref, gate_ref, up_ref, down_ref, og, sem):
+    step = pl.program_id(0)
+
+    def fetch():
+        return pltpu.make_async_copy(o_ref, og, sem)
+
+    @pl.when(step == 0)
+    def _():
+        fetch().start()
+
+    @pl.when(step < DOWN)
+    def _():
+        down_ref[...] = jnp.dot(ht_ref[...], c_ref[...].reshape(1024, 512), preferred_element_type=F32)
+
+    @pl.when(step == DOWN)
+    def _():
+        fetch().wait()
+
+    @pl.when((step >= DOWN) & (step < DOWN + 2))
+    def _():
+        gate_ref[...] = jnp.dot(xt_ref[...], og[:, :, :, 0].reshape(1024, 2 * HALF), preferred_element_type=F32)
+
+    @pl.when(step >= DOWN + 2)
+    def _():
+        up_ref[...] = jnp.dot(xt_ref[...], og[:, :, :, 1].reshape(1024, 2 * HALF), preferred_element_type=F32)
+
+
+DOWN = 4
 
 
 def grads_call(xt, c, ht, o):
-    width = 256
     n = CHUNKS
-    part = lambda m: pl.BlockSpec((n, 4, 2, 1, 16, width), lambda j: (0, 0, 0, m, 0, j))
+    rows = 2 * HALF // DOWN
+    down = lambda j: (jnp.minimum(j, DOWN - 1), 0)
+    gate = lambda j: (jnp.clip(j - DOWN, 0, 1), 0)
+    up = lambda j: (jnp.clip(j - DOWN - 2, 0, 1), 0)
     return pl.pallas_call(
         grads_kernel,
-        grid=(1792 // width,),
+        grid=(DOWN + 4,),
         out_shape=(
-            jax.ShapeDtypeStruct((512, 1792), F32),
-            jax.ShapeDtypeStruct((512, 1792), F32),
-            jax.ShapeDtypeStruct((1792, 512), F32),
+            jax.ShapeDtypeStruct((512, 2 * HALF), F32),
+            jax.ShapeDtypeStruct((512, 2 * HALF), F32),
+            jax.ShapeDtypeStruct((2 * HALF, 512), F32),
         ),
         in_specs=[
-            pl.BlockSpec((512, 1024), lambda j: (0, 0)),
+            pl.BlockSpec((256, 1024), lambda j: (jnp.maximum(j - DOWN, 0) % 2, 0)),
             pl.BlockSpec((n, 128, 512), lambda j: (0, 0, 0)),
-            pl.BlockSpec((width, 1024), lambda j: (j, 0)),
-            part(0), part(1),
+            pl.BlockSpec((rows, 1024), down),
+            pl.BlockSpec(memory_space=pl.ANY),
         ],
         out_specs=(
-            pl.BlockSpec((512, width), lambda j: (0, j)),
-            pl.BlockSpec((512, width), lambda j: (0, j)),
-            pl.BlockSpec((width, 512), lambda j: (j, 0)),
+            pl.BlockSpec((256, 2 * HALF), gate),
+            pl.BlockSpec((256, 2 * HALF), up),
+            pl.BlockSpec((rows, 512), down),
         ),
+        scratch_shapes=[pltpu.VMEM((n, 4, 2, 2, 16, 2 * HALF), BF), pltpu.SemaphoreType.DMA],
         compiler_params=pltpu.CompilerParams(vmem_limit_bytes=60 << 20),
         cost_estimate=pl.CostEstimate(flops=6 * 10**9, bytes_accessed=24 * 10**6, transcendentals=0),
         name="weight_grads",
-    )(xt, c, ht, o, o)
+    )(xt, c, ht, o)
 
 
 def local(vision_tokens, image_counts, image_owner, gate_weight, up_weight, down_weight, out_grad):

time: 141 us -> 139 us (0.986)
    pallas_call x1, Pallas kernels: 125 us -> 122 us  [main_call(): pl.pallas_call(main_kernel, out_shape=(jax.ShapeDtypeStruct((128, 512), B...]
    pallas_call x1, Pallas kernels: 12 us -> 14.4 us  [grads_call(): pl.pallas_call(grads_kernel, grid=(DOWN + 4,), out_shape=(jax.ShapeDtypeS...]
where the time goes in v4:
time: 139 us; the launch traced here: 137 us
  Pallas kernels  136 us (98%)
    pallas_call x1, Pallas kernels, main_call(): pl.pallas_call(main_kernel, out_shape=(jax.ShapeDtypeStruct((128, 512), B...  122 us
    pallas_call x1, Pallas kernels, grads_call(): pl.pallas_call(grads_kernel, grid=(DOWN + 4,), out_shape=(jax.ShapeDtypeS...  14.4 us

profile of v4, /device:TPU:1, one launch (start us, length us, event | category | flops | bytes accessed | tf_op | source)
XLA Modules:
  0.0 137.4 jit_solution(2059898193724115335)
XLA Ops:
  0.6 121.7 %row_sums.1 = (bf16[128,512]{1,0:T(8,128)(2,1)}, bf16[8,4,2,2,16,1792]{5,4,3,2,1,0:T(8,128)(2,1)}, bf16[1792,1024]{1,0:T(8,128)(2,1)}, bf16[512,1024]{1,0:T(8,128)(2,1)}, bf16[8,128,512]{2,1,0:T(8,128)(2,1)}) custom-call(bf16[16,8192]{1,0:T(8,128)(2,1)} %v_ref.1, s32[1,64]{1,0:T(1,128)} %bitcast.2, s32[1,128]{1,0:T(1,128)} %bitcast.3, ...), custom_call_target="tpu_custom_call" | custom-call | flops 10000000000 | bytes 30000000 | tf_op jit(solution)/shard_map/row_sums/pallas_call | solution.py:596
  122.3 0.0 copy-start
  122.3 14.4 %weight_grads.1 = (f32[512,1792]{1,0:T(8,128)}, f32[512,1792]{1,0:T(8,128)}, f32[1792,512]{1,0:T(8,128)}) custom-call(bf16[512,1024]{1,0:T(8,128)(2,1)} %get-tuple-element.13.xt_ref, bf16[8,128,512]{2,1,0:T(8,128)(2,1)} %get-tuple-element.14.c_ref, bf16[1792,1024]{1,0:T(8,128)(2,1)} %get-tuple-element.15.ht_ref, ...), custom_call_target="tpu_custom_call" | custom-call | flops 6000000000 | bytes 24000000 | tf_op jit(solution)/shard_map/weight_grads/pallas_call | solution.py:662
  136.7 0.0 copy-done
  136.7 0.7 copy.12
Async XLA Ops:
  122.3 14.4 %copy-start = (bf16[128,512]{1,0:T(8,128)(2,1)S(1)}, bf16[128,512]{1,0:T(8,128)(2,1)}, u32[]{:S(2)}) copy-start(bf16[128,512]{1,0:T(8,128)(2,1)} %get-tuple-element.24) | copy-start | bytes 393220

commit v5 on v4

--- a/solution.py
+++ b/solution.py
@@ -25,7 +25,7 @@
 WG, WU, WD, LOY, AXL, AYL = range(26, 32)
 ONCE = 32
 SLOTS = 4
-FIRST = 5
+FIRST = 4
 
 def rem(a, n):
     return lax.rem(a, n)
@@ -47,7 +47,7 @@
     *rest,
 ):
     gu, hg = RowSum(0, rest[:18]), RowSum(HG, rest[18:36])
-    ssem, rsem, zsem, ssem1, rsem1, asem, osem, lsem = rest[36:]
+    ssem, rsem, hsem, ssem1, rsem1, asem, osem, lsem = rest[36:]
     row = lax.axis_index("row")
     col = lax.axis_index("col")
     x, y, k = row // 4, rem(row // 2, 2), rem(row, 2)
@@ -91,9 +91,16 @@
     cx = pl.ds(pl.multiple_of(k * HALF, 128), XW)
     cy = pl.ds(pl.multiple_of(k * HALF + XW, 128), YW)
 
+    def landing(kind, t):
+        if HG <= kind < AXY:
+            return hsem.at[kind - HG, t]
+        if kind in (CIN, LOZ):
+            return hsem.at[8 + (kind == LOZ), t]
+        return rsem.at[kind, rem(t, SLOTS)]
+
     def copy(kind, t, src, dst, dev):
         return pltpu.make_async_remote_copy(
-            src_ref=src, dst_ref=dst, send_sem=ssem.at[kind], recv_sem=rsem.at[kind, rem(t, SLOTS)] if kind != LOZ else zsem.at[t],
+            src_ref=src, dst_ref=dst, send_sem=ssem.at[kind], recv_sem=landing(kind, t),
             device_id=dev, device_id_type=MESH,
         )
 
@@ -162,13 +169,16 @@
         return rem(x + s + 4, 4), rem(x - s + 4, 4)
 
     def tokh(u):
-        there = jnp.where((u >= 2) & (u < 6), ho, yh)
-        off = jnp.where((u == 1) | (u == 3), 1, 0)
-        off = off + jnp.where((u == 4) | (u == 6), 3, 0) + jnp.where((u == 5) | (u == 7), 2, 0)
+        there = jnp.where((u < 3) | (u == 6), yh, ho)
+        off = jnp.where((u == 1) | (u == 4), 1, 0)
+        off = off + jnp.where((u == 2) | (u == 5), 3, 0) + jnp.where(u >= 6, 2, 0)
         return there * 4 + rem(z + off, 4)
 
     def tok(t):
-        return tokh(rem(t + 1, 8))
+        there = jnp.where((t >= 1) & (t < 5), ho, yh)
+        off = jnp.where((t == 0) | (t == 2), 1, 0)
+        off = off + jnp.where((t == 3) | (t == 5), 3, 0) + jnp.where((t == 4) | (t == 6), 2, 0)
+        return there * 4 + rem(z + off, 4)
 
     def tokens(c):
         return pl.ds(pl.multiple_of(c * 128, 128), 128)
@@ -214,7 +224,7 @@
             copy(kind, t, place, place, y_dev).wait_recv()
 
     def r0(r, t, parts):
-        b = rem(t, 4)
+        b = t
         ahead, _ = sides(t)
         for m, g in enumerate(parts):
             r.px[b, :, m] = g[:, :XW].reshape(4, 32, XW)
@@ -228,7 +238,7 @@
         start(t, r.base + YY)
 
     def r1(r, t):
-        b = rem(t, 4)
+        b = t
         ahead, back = sides(t)
         arrive(t, r.base + XR)
         r.sx2[t] = (r.px[b, back] + r.rxr[t].astype(F32)).astype(BF)
@@ -240,7 +250,7 @@
         start(t, r.base + YD, r.base + YR)
 
     def r2(r, t):
-        b = rem(t, 4)
+        b = t
         _, back = sides(t)
         arrive(t, r.base + XD, r.base + X2)
         r.px[b, x] = r.px[b, x] + r.rxd[t].astype(F32) + r.rx2[t].astype(F32)
@@ -251,12 +261,12 @@
         start(t, r.base + Y2)
 
     def r3x(r, t):
-        b = rem(t, 4)
+        b = t
         arrive(t, r.base + XY)
         return r.px[b, x, :, pl.ds(pl.multiple_of(y * 16, 16), 16), :] + r.rxy[t].astype(F32)
 
     def r3y(r, t):
-        b = rem(t, 4)
+        b = t
         arrive(t, r.base + YD, r.base + Y2)
         return r.py[b, y, x] + r.ryd[t].astype(F32) + r.ry2[t].astype(F32)
 
@@ -470,22 +480,29 @@
     def c_0():
         arrive1(CM)
         start1(CF2)
+        arrive1(CP)
+        start1(CF1)
+        start(1, CIN)
+        start(2, CIN)
         arrive1(CY)
         start1(DP, DM)
-        arrive1(CP)
-        start1(CF1)
-
-    def c_2():
+        start(3, CIN)
+
+    def c_1():
+        arrive1(DM)
+        start1(DF2)
         arrive1(DP)
         start1(DF1)
-        arrive1(DM)
-        start1(DF2)
-
-    def c_4():
+        start(4, CIN)
+
+    def c_2():
+        arrive1(CF1, CF2)
+        start(5, CIN)
+        start(6, CIN)
+
+    def c_3():
         arrive1(DF1, DF2)
-
-    def c_6():
-        arrive1(CF1, CF2)
+        start(7, CIN)
         pltpu.make_async_copy(c2.at[:, :, 0:512], co_ref, lsem.at[4]).start()
 
     def w_0():
@@ -521,16 +538,12 @@
     def step(n, carry):
         at(n, 0, w_0)
         for lag, stage in enumerate([h0, lambda u: r1(hg, u), lambda u: r2(hg, u), h3]):
-            each(n, lag, stage)
+            each(2 * (n - lag) - 1, 0, stage)
+            each(2 * (n - lag), 0, stage)
         at(n, 0, c_0)
+        at(n, 1, c_1)
         at(n, 2, c_2)
-        at(n, 4, c_4)
-        at(n, 6, c_6)
-
-        @pl.when(n < CHUNKS - 1)
-        def _():
-            start(n + 1, CIN)
-
+        at(n, 3, c_3)
         at(n, 0, v_0)
         at(n, 2, v_2)
         at(n, 3, v_3)
@@ -588,7 +601,7 @@
     def row_sum(mats):
         xb, xq, yb = (n, mats, 32, XW), (n, mats, 16, XW), (n, mats, 16, YW)
         moves = [vm(*xb), vm(*xb), vm(*xb), vm(*xq), vm(n, 4, mats, 16, YW), vm(*yb), vm(*yb), vm(*yb)]
-        return [vf(4, 4, mats, 32, XW), vf(4, 2, 4, mats, 16, YW), *moves, *moves]
+        return [vf(8, 4, mats, 32, XW), vf(8, 2, 4, mats, 16, YW), *moves, *moves]
 
     dma = pltpu.SemaphoreType.DMA
     vmem = pl.BlockSpec(memory_space=pltpu.VMEM)
@@ -612,7 +625,7 @@
             vf(n, 16, XW), vf(n, 16, YW),
             vf(n, 128, 512), vf(n, 128, 512), vf(128, 512), vf(128, 512),
             *row_sum(2), *row_sum(1),
-            dma((KINDS,)), dma((KINDS, SLOTS)), dma((n,)), dma((ONCE,)), dma((ONCE,)), dma((2,)),
+            dma((KINDS,)), dma((KINDS, SLOTS)), dma((10, n)), dma((ONCE,)), dma((ONCE,)), dma((2,)),
             dma((3,)), dma((5,)),
         ],
         compiler_params=pltpu.CompilerParams(
@@ -623,64 +636,57 @@
     )(v, counts, owner, og, gate, up, down)
 
 
-def grads_kernel(xt_ref, c_ref, ht_ref, o_ref, gate_ref, up_ref, down_ref, og, sem):
-    step = pl.program_id(0)
-
-    def fetch():
-        return pltpu.make_async_copy(o_ref, og, sem)
-
-    @pl.when(step == 0)
-    def _():
-        fetch().start()
-
-    @pl.when(step < DOWN)
-    def _():
-        down_ref[...] = jnp.dot(ht_ref[...], c_ref[...].reshape(1024, 512), preferred_element_type=F32)
-
-    @pl.when(step == DOWN)
-    def _():
-        fetch().wait()
-
-    @pl.when((step >= DOWN) & (step < DOWN + 2))
-    def _():
-        gate_ref[...] = jnp.dot(xt_ref[...], og[:, :, :, 0].reshape(1024, 2 * HALF), preferred_element_type=F32)
-
-    @pl.when(step >= DOWN + 2)
-    def _():
-        up_ref[...] = jnp.dot(xt_ref[...], og[:, :, :, 1].reshape(1024, 2 * HALF), preferred_element_type=F32)
-
-
-DOWN = 4
+def grads_kernel(xt_hbm, c_hbm, ht_hbm, o_hbm, gate_hbm, up_hbm, down_hbm, xt, c, ht, o, gate, up, down, lsem, wsem):
+    load = pltpu.make_async_copy
+    strips = [slice(0, HALF), slice(HALF, 2 * HALF)]
+    x_in, c_in = load(xt_hbm, xt, lsem.at[0]), load(c_hbm, c, lsem.at[1])
+    ht_in = [load(ht_hbm.at[s], ht.at[s], lsem.at[2 + i]) for i, s in enumerate(strips)]
+    o_in = [
+        [load(o_hbm.at[:, :, :, m, :, s], o.at[:, :, :, m, :, s], lsem.at[4 + 2 * i + m]) for m in range(2)]
+        for i, s in enumerate(strips)
+    ]
+    c_in.start()
+    ht_in[0].start()
+    x_in.start()
+    for copies in (o_in[0], ht_in[1:], o_in[1]):
+        for copy in copies:
+            copy.start()
+    out = []
+
+    def write(src, dst):
+        out.append(pltpu.make_async_copy(src, dst, wsem.at[len(out)]))
+        out[-1].start()
+
+    c_in.wait()
+    for i, s in enumerate(strips):
+        ht_in[i].wait()
+        down[s] = jnp.dot(ht[s], c[...].reshape(1024, 512), preferred_element_type=F32)
+        write(down.at[s], down_hbm.at[s])
+        if i == 0:
+            x_in.wait()
+        for m, (grad, hbm) in enumerate(((gate, gate_hbm), (up, up_hbm))):
+            o_in[i][m].wait()
+            grad[:, s] = jnp.dot(xt[...], o[:, :, :, m, :, s].reshape(1024, HALF), preferred_element_type=F32)
+            write(grad.at[:, s], hbm.at[:, s])
+    for copy in out:
+        copy.wait()
 
 
 def grads_call(xt, c, ht, o):
-    n = CHUNKS
-    rows = 2 * HALF // DOWN
-    down = lambda j: (jnp.minimum(j, DOWN - 1), 0)
-    gate = lambda j: (jnp.clip(j - DOWN, 0, 1), 0)
-    up = lambda j: (jnp.clip(j - DOWN - 2, 0, 1), 0)
+    hbm = pl.BlockSpec(memory_space=pl.ANY)
+    up, down = (512, 2 * HALF), (2 * HALF, 512)
     return pl.pallas_call(
         grads_kernel,
-        grid=(DOWN + 4,),
-        out_shape=(
-            jax.ShapeDtypeStruct((512, 2 * HALF), F32),
-            jax.ShapeDtypeStruct((512, 2 * HALF), F32),
-            jax.ShapeDtypeStruct((2 * HALF, 512), F32),
-        ),
-        in_specs=[
-            pl.BlockSpec((256, 1024), lambda j: (jnp.maximum(j - DOWN, 0) % 2, 0)),
-            pl.BlockSpec((n, 128, 512), lambda j: (0, 0, 0)),
-            pl.BlockSpec((rows, 1024), down),
-            pl.BlockSpec(memory_space=pl.ANY),
+        out_shape=tuple(jax.ShapeDtypeStruct(shape, F32) for shape in (up, up, down)),
+        in_specs=[hbm] * 4,
+        out_specs=(hbm, hbm, hbm),
+        scratch_shapes=[
+            *(pltpu.VMEM(a.shape, BF) for a in (xt, c, ht, o)),
+            *(pltpu.VMEM(shape, F32) for shape in (up, up, down)),
+            pltpu.SemaphoreType.DMA((8,)), pltpu.SemaphoreType.DMA((6,)),
         ],
-        out_specs=(
-            pl.BlockSpec((256, 2 * HALF), gate),
-            pl.BlockSpec((256, 2 * HALF), up),
-            pl.BlockSpec((rows, 512), down),
-        ),
-        scratch_shapes=[pltpu.VMEM((n, 4, 2, 2, 16, 2 * HALF), BF), pltpu.SemaphoreType.DMA],
         compiler_params=pltpu.CompilerParams(vmem_limit_bytes=60 << 20),
-        cost_estimate=pl.CostEstimate(flops=6 * 10**9, bytes_accessed=24 * 10**6, transcendentals=0),
+        cost_estimate=pl.CostEstimate(flops=8 * 10**9, bytes_accessed=24 * 10**6, transcendentals=0),
         name="weight_grads",
     )(xt, c, ht, o)
 

time: 139 us -> 134 us (0.964)
  Pallas kernels: 136 us -> 132 us
    pallas_call x1, Pallas kernels: 14.4 us -> 10.4 us  [grads_call(): pl.pallas_call(grads_kernel, out_shape=tuple((jax.ShapeDtypeStruct(shape,...]
where the time goes in v5:
time: 134 us
  Pallas kernels  132 us (99%)
    pallas_call x1, Pallas kernels, main_call(): pl.pallas_call(main_kernel, out_shape=(jax.ShapeDtypeStruct((128, 512), B...  122 us
    pallas_call x1, Pallas kernels, grads_call(): pl.pallas_call(grads_kernel, out_shape=tuple((jax.ShapeDtypeStruct(shape,...  10.4 us

profile of v5, /device:TPU:1, one launch (start us, length us, event | category | flops | bytes accessed | tf_op | source)
XLA Modules:
  0.0 133.5 jit_solution(16941973036777039264)
XLA Ops:
  0.6 121.8 %row_sums.1 = (bf16[128,512]{1,0:T(8,128)(2,1)}, bf16[8,4,2,2,16,1792]{5,4,3,2,1,0:T(8,128)(2,1)}, bf16[1792,1024]{1,0:T(8,128)(2,1)}, bf16[512,1024]{1,0:T(8,128)(2,1)}, bf16[8,128,512]{2,1,0:T(8,128)(2,1)}) custom-call(bf16[16,8192]{1,0:T(8,128)(2,1)} %v_ref.1, s32[1,64]{1,0:T(1,128)} %bitcast.2, s32[1,128]{1,0:T(1,128)} %bitcast.3, ...), custom_call_target="tpu_custom_call" | custom-call | flops 10000000000 | bytes 30000000 | tf_op jit(solution)/shard_map/row_sums/pallas_call | solution.py:609
  122.4 0.0 copy-start
  122.4 10.4 %weight_grads.1 = (f32[512,1792]{1,0:T(8,128)}, f32[512,1792]{1,0:T(8,128)}, f32[1792,512]{1,0:T(8,128)}) custom-call(bf16[512,1024]{1,0:T(8,128)(2,1)} %get-tuple-element.13.xt_hbm, bf16[8,128,512]{2,1,0:T(8,128)(2,1)} %get-tuple-element.14.c_hbm, bf16[1792,1024]{1,0:T(8,128)(2,1)} %get-tuple-element.15.ht_hbm, ...), custom_call_target="tpu_custom_call" | custom-call | flops 8000000000 | bytes 24000000 | tf_op jit(solution)/shard_map/weight_grads/pallas_call | solution.py:678
  132.9 0.0 copy-done
  132.9 0.7 copy.12
Async XLA Ops:
  122.4 10.5 %copy-start = (bf16[128,512]{1,0:T(8,128)(2,1)S(1)}, bf16[128,512]{1,0:T(8,128)(2,1)}, u32[]{:S(2)}) copy-start(bf16[128,512]{1,0:T(8,128)(2,1)} %get-tuple-element.24) | copy-start | bytes 393220

commit v6 on v5

--- a/solution.py
+++ b/solution.py
@@ -22,8 +22,8 @@
 CP, CM, CY, CF1, CF2, DP, DM, DF1, DF2 = range(9)
 TP, TM, TY, TF1, TF2, UP, UM, UF1, UF2 = range(9, 18)
 RZ1, RZ2, RZ3, RZY, RY, RYZ1, RYZ2, RYZ3 = range(18, 26)
-WG, WU, WD, LOY, AXL, AYL = range(26, 32)
-ONCE = 32
+WG, WU, WD, LOY, AXL, AYL, LO6 = range(26, 33)
+ONCE = 33
 SLOTS = 4
 FIRST = 4
 
@@ -43,7 +43,7 @@
     out_ref, o_ref, ht_ref, xt_ref, co_ref,
     act, pool, xin, c2, wg, wu, wd, wdo,
     hot, part, rtz, rty, stz, rtyz, rtzy, ht, xt,
-    hfx, hfy, lo, rz, zs, rh,
+    hfx, hfy, lo, rz, zs, rh, lo6, rz6,
     *rest,
 ):
     gu, hg = RowSum(0, rest[:18]), RowSum(HG, rest[18:36])
@@ -94,9 +94,9 @@
     def landing(kind, t):
         if HG <= kind < AXY:
             return hsem.at[kind - HG, t]
-        if kind in (CIN, LOZ):
-            return hsem.at[8 + (kind == LOZ), t]
-        return rsem.at[kind, rem(t, SLOTS)]
+        if kind in (CIN, LOZ, CORE):
+            return hsem.at[8 + (CIN, LOZ, CORE).index(kind), t]
+        return rsem.at[kind if kind < HG else kind - AXY + HG, rem(t, SLOTS)]
 
     def copy(kind, t, src, dst, dev):
         return pltpu.make_async_remote_copy(
@@ -150,6 +150,7 @@
         RYZ2: lambda: (part.at[yh, zf, :, 256:512], rtyz.at[1], at_col(yh, zf), rtyz.at[1]),
         RYZ3: lambda: (part.at[yh, zm, :, 256:512], rtyz.at[2], at_col(yh, zm), rtyz.at[2]),
         LOY: lambda: (zs, rh, hi_dev, rh),
+        LO6: lambda: (lo6, rz6, at_col(yh, zf), rz6),
         AXL: lambda: (*same(act.at[col, x, :, :, :, cx]), far_dev, act.at[col, far, :, :, :, cx]),
         AYL: lambda: (*same(act.at[col, x, y, :, :, cy]), far_dev, act.at[col, far, y, :, :, cy]),
     }
@@ -169,9 +170,9 @@
         return rem(x + s + 4, 4), rem(x - s + 4, 4)
 
     def tokh(u):
-        there = jnp.where((u < 3) | (u == 6), yh, ho)
-        off = jnp.where((u == 1) | (u == 4), 1, 0)
-        off = off + jnp.where((u == 2) | (u == 5), 3, 0) + jnp.where(u >= 6, 2, 0)
+        there = jnp.where((u < 3) | (u == 4), yh, ho)
+        off = jnp.where((u == 1) | (u == 5), 1, 0)
+        off = off + jnp.where((u == 2) | (u == 6), 3, 0) + jnp.where((u == 4) | (u == 7), 2, 0)
         return there * 4 + rem(z + off, 4)
 
     def tok(t):
@@ -446,9 +447,14 @@
         hidden = act[c, :, :, 0].reshape(128, 2 * HALF)
         lo[t] = jnp.dot(hidden, wdo[...], preferred_element_type=F32)
 
-        @pl.when((t != 1) & (t != 7))
+        @pl.when((t != 1) & (t < 6))
         def _():
             start(t, LOZ)
+
+        @pl.when(t == 6)
+        def _():
+            lo6[...] = lo[6].astype(BF)
+            start1(LO6)
 
         ht[t] = hidden.T
         pltpu.make_async_copy(ht.at[t], ht_ref.at[:, tokens(c)], osem.at[2]).start()
@@ -484,23 +490,25 @@
         start1(CF1)
         start(1, CIN)
         start(2, CIN)
+
+    def c_1():
         arrive1(CY)
+        start(3, CIN)
+        arrive1(CF1, CF2)
+        start(4, CIN)
+
+    def c_2():
         start1(DP, DM)
-        start(3, CIN)
-
-    def c_1():
+
+    def c_3():
         arrive1(DM)
         start1(DF2)
         arrive1(DP)
         start1(DF1)
-        start(4, CIN)
-
-    def c_2():
-        arrive1(CF1, CF2)
         start(5, CIN)
         start(6, CIN)
 
-    def c_3():
+    def c_4():
         arrive1(DF1, DF2)
         start(7, CIN)
         pltpu.make_async_copy(c2.at[:, :, 0:512], co_ref, lsem.at[4]).start()
@@ -538,15 +546,18 @@
     def step(n, carry):
         at(n, 0, w_0)
         for lag, stage in enumerate([h0, lambda u: r1(hg, u), lambda u: r2(hg, u), h3]):
-            each(2 * (n - lag) - 1, 0, stage)
-            each(2 * (n - lag), 0, stage)
+            q = n - lag
+            m = jnp.where(q == 3, -1, jnp.where(q > 3, q - 1, q))
+            each(2 * m - 1, 0, stage)
+            each(2 * m, 0, stage)
         at(n, 0, c_0)
         at(n, 1, c_1)
-        at(n, 2, c_2)
-        at(n, 3, c_3)
         at(n, 0, v_0)
         at(n, 2, v_2)
+        at(n, 2, c_2)
         at(n, 3, v_3)
+        at(n, 3, c_3)
+        at(n, 4, c_4)
         at(n, FIRST, t_0)
         at(n, FIRST + 2, t_2)
         at(n, FIRST + 4, t_4)
@@ -562,9 +573,9 @@
     lax.fori_loop(0, FIRST + CHUNKS + 7, step, 0)
     arrive(0, LOZ)
     arrive(5, LOZ)
-    arrive(6, LOZ)
     arrive1(LOY)
-    out_ref[...] = (lo[7] + rz[0] + rz[5] + rz[6] + rh[...]).astype(BF)
+    arrive1(LO6)
+    out_ref[...] = (lo[7] + rz[0] + rz[5] + rz6[...].astype(F32) + rh[...]).astype(BF)
 
     def all_sent(kind):
         if kind < 16:
@@ -577,7 +588,7 @@
         return {
             AXY: lambda: act.at[:, x, y, :, :, cx], AYY: lambda: act.at[:, :, y, :, :, cy],
             CORE: lambda: act.at[:, :, :, :, :, mine], XIN: lambda: xin.at[:, :, 0:512],
-            CIN: lambda: c2.at[:, :, 0:512], LOZ: lambda: lo.at[0:6],
+            CIN: lambda: c2.at[:, :, 0:512], LOZ: lambda: lo.at[0:5],
         }[kind]()
 
     for kind in range(KINDS):
@@ -623,9 +634,9 @@
             vm(8, 128, 256), vm(2, 4, 128, 512), vm(3, 2, 128, 256), vm(4, 128, 256), vm(128, 256), vm(3, 128, 256), vm(128, 256),
             vm(n, 2 * HALF, 128), vm(n, 512, 128),
             vf(n, 16, XW), vf(n, 16, YW),
-            vf(n, 128, 512), vf(n, 128, 512), vf(128, 512), vf(128, 512),
+            vf(n, 128, 512), vf(n, 128, 512), vf(128, 512), vf(128, 512), vm(128, 512), vm(128, 512),
             *row_sum(2), *row_sum(1),
-            dma((KINDS,)), dma((KINDS, SLOTS)), dma((10, n)), dma((ONCE,)), dma((ONCE,)), dma((2,)),
+            dma((KINDS,)), dma((18, SLOTS)), dma((11, n)), dma((ONCE,)), dma((ONCE,)), dma((2,)),
             dma((3,)), dma((5,)),
         ],
         compiler_params=pltpu.CompilerParams(
@@ -636,7 +647,7 @@
     )(v, counts, owner, og, gate, up, down)
 
 
-def grads_kernel(xt_hbm, c_hbm, ht_hbm, o_hbm, gate_hbm, up_hbm, down_hbm, xt, c, ht, o, gate, up, down, lsem, wsem):
+def grads_kernel(xt_hbm, c_hbm, ht_hbm, o_hbm, y_hbm, gate_hbm, up_hbm, down_hbm, out_hbm, xt, c, ht, o, gate, up, down, lsem, wsem):
     load = pltpu.make_async_copy
     strips = [slice(0, HALF), slice(HALF, 2 * HALF)]
     x_in, c_in = load(xt_hbm, xt, lsem.at[0]), load(c_hbm, c, lsem.at[1])
@@ -657,6 +668,7 @@
         out.append(pltpu.make_async_copy(src, dst, wsem.at[len(out)]))
         out[-1].start()
 
+    write(y_hbm, out_hbm)
     c_in.wait()
     for i, s in enumerate(strips):
         ht_in[i].wait()
@@ -672,30 +684,33 @@
         copy.wait()
 
 
-def grads_call(xt, c, ht, o):
+def grads_call(xt, c, ht, o, y):
     hbm = pl.BlockSpec(memory_space=pl.ANY)
     up, down = (512, 2 * HALF), (2 * HALF, 512)
     return pl.pallas_call(
         grads_kernel,
-        out_shape=tuple(jax.ShapeDtypeStruct(shape, F32) for shape in (up, up, down)),
-        in_specs=[hbm] * 4,
-        out_specs=(hbm, hbm, hbm),
+        out_shape=(
+            *(jax.ShapeDtypeStruct(shape, F32) for shape in (up, up, down)),
+            jax.ShapeDtypeStruct(y.shape, y.dtype),
+        ),
+        in_specs=[hbm] * 5,
+        out_specs=(hbm, hbm, hbm, hbm),
         scratch_shapes=[
             *(pltpu.VMEM(a.shape, BF) for a in (xt, c, ht, o)),
             *(pltpu.VMEM(shape, F32) for shape in (up, up, down)),
-            pltpu.SemaphoreType.DMA((8,)), pltpu.SemaphoreType.DMA((6,)),
+            pltpu.SemaphoreType.DMA((8,)), pltpu.SemaphoreType.DMA((7,)),
         ],
         compiler_params=pltpu.CompilerParams(vmem_limit_bytes=60 << 20),
         cost_estimate=pl.CostEstimate(flops=8 * 10**9, bytes_accessed=24 * 10**6, transcendentals=0),
         name="weight_grads",
-    )(xt, c, ht, o)
+    )(xt, c, ht, o, y)
 
 
 def local(vision_tokens, image_counts, image_owner, gate_weight, up_weight, down_weight, out_grad):
-    layer_out, o, ht, xt, c = main_call(
+    y, o, ht, xt, c = main_call(
         vision_tokens, image_counts[None, :], image_owner[None, :], out_grad, gate_weight, up_weight, down_weight
     )
-    grad_gate, grad_up, grad_down = grads_call(xt, c, ht, o)
+    grad_gate, grad_up, grad_down, layer_out = grads_call(xt, c, ht, o, y)
     return (layer_out, grad_gate, grad_up, grad_down)
 
 

time: 134 us -> 130 us (0.970)
  Pallas kernels: 132 us -> 129 us
    pallas_call x1, Pallas kernels: 122 us -> 118 us  [main_call(): pl.pallas_call(main_kernel, out_shape=(jax.ShapeDtypeStruct((128, 512), B...]
where the time goes in v6:
time: 130 us; the launch traced here: 129 us
  Pallas kernels  129 us (99%)
    pallas_call x1, Pallas kernels, main_call(): pl.pallas_call(main_kernel, out_shape=(jax.ShapeDtypeStruct((128, 512), B...  118 us
    pallas_call x1, Pallas kernels, grads_call(): pl.pallas_call(grads_kernel, out_shape=(*(jax.ShapeDtypeStruct(shape, F32...  10.4 us

profile of v6, /device:TPU:1, one launch (start us, length us, event | category | flops | bytes accessed | tf_op | source)
XLA Modules:
  0.0 129.4 jit_solution(17341201712925209384)
XLA Ops:
  0.6 118.4 %row_sums.1 = (bf16[128,512]{1,0:T(8,128)(2,1)}, bf16[8,4,2,2,16,1792]{5,4,3,2,1,0:T(8,128)(2,1)}, bf16[1792,1024]{1,0:T(8,128)(2,1)}, bf16[512,1024]{1,0:T(8,128)(2,1)}, bf16[8,128,512]{2,1,0:T(8,128)(2,1)}) custom-call(bf16[16,8192]{1,0:T(8,128)(2,1)} %v_ref.1, s32[1,64]{1,0:T(1,128)} %bitcast.2, s32[1,128]{1,0:T(1,128)} %bitcast.3, ...), custom_call_target="tpu_custom_call" | custom-call | flops 10000000000 | bytes 30000000 | tf_op jit(solution)/shard_map/row_sums/pallas_call | solution.py:620
  119.0 10.4 %weight_grads.1 = (f32[512,1792]{1,0:T(8,128)}, f32[512,1792]{1,0:T(8,128)}, f32[1792,512]{1,0:T(8,128)}, bf16[128,512]{1,0:T(8,128)(2,1)}) custom-call(bf16[512,1024]{1,0:T(8,128)(2,1)} %get-tuple-element.13.xt_hbm, bf16[8,128,512]{2,1,0:T(8,128)(2,1)} %get-tuple-element.14.c_hbm, bf16[1792,1024]{1,0:T(8,128)(2,1)} %get-tuple-element.15.ht_hbm, ...), custom_call_target="tpu_custom_call" | custom-call | flops 8000000000 | bytes 24000000 | tf_op jit(solution)/shard_map/weight_grads/pallas_call | solution.py:690

commit v7 on v6

--- a/solution.py
+++ b/solution.py
@@ -92,11 +92,11 @@
     cy = pl.ds(pl.multiple_of(k * HALF + XW, 128), YW)
 
     def landing(kind, t):
-        if HG <= kind < AXY:
-            return hsem.at[kind - HG, t]
+        if kind < AXY:
+            return hsem.at[kind, t]
         if kind in (CIN, LOZ, CORE):
-            return hsem.at[8 + (CIN, LOZ, CORE).index(kind), t]
-        return rsem.at[kind if kind < HG else kind - AXY + HG, rem(t, SLOTS)]
+            return hsem.at[16 + (CIN, LOZ, CORE).index(kind), t]
+        return rsem.at[kind - AXY, rem(t, SLOTS)]
 
     def copy(kind, t, src, dst, dev):
         return pltpu.make_async_remote_copy(
@@ -564,13 +564,13 @@
         at(n, FIRST + 6, t_6)
         at(n, FIRST + 1, w_1)
         for lag, stage in [
-            (0, p0), (1, s0), (2, lambda t: r1(gu, t)), (3, lambda t: r2(gu, t)), (4, s3), (5, s4), (6, s5),
-            (8, s7), (7, s6), (9, s8),
+            (0, p0), (1, s0), (2, lambda t: r1(gu, t)), (4, lambda t: r2(gu, t)), (6, s3), (7, s4), (8, s5),
+            (10, s7), (9, s6), (11, s8),
         ]:
             each(n, FIRST + lag, stage)
         return carry
 
-    lax.fori_loop(0, FIRST + CHUNKS + 7, step, 0)
+    lax.fori_loop(0, FIRST + CHUNKS + 9, step, 0)
     arrive(0, LOZ)
     arrive(5, LOZ)
     arrive1(LOY)
@@ -636,7 +636,7 @@
             vf(n, 16, XW), vf(n, 16, YW),
             vf(n, 128, 512), vf(n, 128, 512), vf(128, 512), vf(128, 512), vm(128, 512), vm(128, 512),
             *row_sum(2), *row_sum(1),
-            dma((KINDS,)), dma((18, SLOTS)), dma((11, n)), dma((ONCE,)), dma((ONCE,)), dma((2,)),
+            dma((KINDS,)), dma((10, SLOTS)), dma((19, n)), dma((ONCE,)), dma((ONCE,)), dma((2,)),
             dma((3,)), dma((5,)),
         ],
         compiler_params=pltpu.CompilerParams(
@@ -650,16 +650,18 @@
 def grads_kernel(xt_hbm, c_hbm, ht_hbm, o_hbm, y_hbm, gate_hbm, up_hbm, down_hbm, out_hbm, xt, c, ht, o, gate, up, down, lsem, wsem):
     load = pltpu.make_async_copy
     strips = [slice(0, HALF), slice(HALF, 2 * HALF)]
+    quarters = [slice(i * HALF // 2, (i + 1) * HALF // 2) for i in range(4)]
     x_in, c_in = load(xt_hbm, xt, lsem.at[0]), load(c_hbm, c, lsem.at[1])
-    ht_in = [load(ht_hbm.at[s], ht.at[s], lsem.at[2 + i]) for i, s in enumerate(strips)]
+    ht_in = [load(ht_hbm.at[s], ht.at[s], lsem.at[2 + i]) for i, s in enumerate(quarters)]
     o_in = [
-        [load(o_hbm.at[:, :, :, m, :, s], o.at[:, :, :, m, :, s], lsem.at[4 + 2 * i + m]) for m in range(2)]
+        [load(o_hbm.at[:, :, :, m, :, s], o.at[:, :, :, m, :, s], lsem.at[6 + 2 * i + m]) for m in range(2)]
         for i, s in enumerate(strips)
     ]
     c_in.start()
     ht_in[0].start()
+    ht_in[1].start()
     x_in.start()
-    for copies in (o_in[0], ht_in[1:], o_in[1]):
+    for copies in (o_in[0], ht_in[2:], o_in[1]):
         for copy in copies:
             copy.start()
     out = []
@@ -671,15 +673,18 @@
     write(y_hbm, out_hbm)
     c_in.wait()
     for i, s in enumerate(strips):
-        ht_in[i].wait()
-        down[s] = jnp.dot(ht[s], c[...].reshape(1024, 512), preferred_element_type=F32)
-        write(down.at[s], down_hbm.at[s])
+        for q in (2 * i, 2 * i + 1):
+            ht_in[q].wait()
+            down[quarters[q]] = jnp.dot(ht[quarters[q]], c[...].reshape(1024, 512), preferred_element_type=F32)
+            write(down.at[quarters[q]], down_hbm.at[quarters[q]])
         if i == 0:
             x_in.wait()
         for m, (grad, hbm) in enumerate(((gate, gate_hbm), (up, up_hbm))):
             o_in[i][m].wait()
-            grad[:, s] = jnp.dot(xt[...], o[:, :, :, m, :, s].reshape(1024, HALF), preferred_element_type=F32)
-            write(grad.at[:, s], hbm.at[:, s])
+            rows = [slice(0, 512)] if i + m < 2 else [slice(0, 256), slice(256, 512)]
+            for r in rows:
+                grad[r, s] = jnp.dot(xt[r], o[:, :, :, m, :, s].reshape(1024, HALF), preferred_element_type=F32)
+                write(grad.at[r, s], hbm.at[r, s])
     for copy in out:
         copy.wait()
 
@@ -698,7 +703,7 @@
         scratch_shapes=[
             *(pltpu.VMEM(a.shape, BF) for a in (xt, c, ht, o)),
             *(pltpu.VMEM(shape, F32) for shape in (up, up, down)),
-            pltpu.SemaphoreType.DMA((8,)), pltpu.SemaphoreType.DMA((7,)),
+            pltpu.SemaphoreType.DMA((10,)), pltpu.SemaphoreType.DMA((10,)),
         ],
         compiler_params=pltpu.CompilerParams(vmem_limit_bytes=60 << 20),
         cost_estimate=pl.CostEstimate(flops=8 * 10**9, bytes_accessed=24 * 10**6, transcendentals=0),

time: 130 us -> 129 us (level)
  no operation moved by 1% of the time
where the time goes in v7:
time: 129 us
  Pallas kernels  129 us (100%)
    pallas_call x1, Pallas kernels, main_call(): pl.pallas_call(main_kernel, out_shape=(jax.ShapeDtypeStruct((128, 512), B...  118 us
    pallas_call x1, Pallas kernels, grads_call(): pl.pallas_call(grads_kernel, out_shape=(*(jax.ShapeDtypeStruct(shape, F32...  10.2 us

profile of v7, /device:TPU:1, one launch (start us, length us, event | category | flops | bytes accessed | tf_op | source)
XLA Modules:
  0.0 129.3 jit_solution(15430131768236056375)
XLA Ops:
  0.6 118.4 %row_sums.1 = (bf16[128,512]{1,0:T(8,128)(2,1)}, bf16[8,4,2,2,16,1792]{5,4,3,2,1,0:T(8,128)(2,1)}, bf16[1792,1024]{1,0:T(8,128)(2,1)}, bf16[512,1024]{1,0:T(8,128)(2,1)}, bf16[8,128,512]{2,1,0:T(8,128)(2,1)}) custom-call(bf16[16,8192]{1,0:T(8,128)(2,1)} %v_ref.1, s32[1,64]{1,0:T(1,128)} %bitcast.2, s32[1,128]{1,0:T(1,128)} %bitcast.3, ...), custom_call_target="tpu_custom_call" | custom-call | flops 10000000000 | bytes 30000000 | tf_op jit(solution)/shard_map/row_sums/pallas_call | solution.py:620
  119.1 10.2 %weight_grads.1 = (f32[512,1792]{1,0:T(8,128)}, f32[512,1792]{1,0:T(8,128)}, f32[1792,512]{1,0:T(8,128)}, bf16[128,512]{1,0:T(8,128)(2,1)}) custom-call(bf16[512,1024]{1,0:T(8,128)(2,1)} %get-tuple-element.13.xt_hbm, bf16[8,128,512]{2,1,0:T(8,128)(2,1)} %get-tuple-element.14.c_hbm, bf16[1792,1024]{1,0:T(8,128)(2,1)} %get-tuple-element.15.ht_hbm, ...), custom_call_target="tpu_custom_call" | custom-call | flops 8000000000 | bytes 24000000 | tf_op jit(solution)/shard_map/weight_grads/pallas_call | solution.py:695
